TPU v7x, 256 devices: a whole 4x4x8 slice. The times are simulated.
256 devices in a mesh: row: 16 (over z, y_hi), col: 16 (over y_lo, x, core).
Axes of the slice: x: 4, y: 4 (y_hi: 2, y_lo: 2; y = y_hi * 2 + y_lo), z: 8, core: 2. Of those that a mesh axis runs over, the one named last changes fastest.
Arguments:
- coarse_kernel: bfloat16 [1024, 1024], P('row', 'col'), may hold values from -0.031488349 to 0.031488349, as said below
- correlations: bfloat16 [256, 128, 128], P(('row', 'col')), may hold values from -0.5 to 0.5
- neighbor: int32 [256], P(('row', 'col')), may hold values from 0 to 7
- pair_weight: float32 [256, 256], P('row'), may hold values from 0.13 to 7.4, as said below
- energies: float32 [32768], P(('row', 'col')), may hold values from 0.5 to 2
- start_block: float32 [32768, 64], P(('row', 'col')), may hold values from -120 to 120
Outputs:
- residual: float32 [32768, 64], P(('row', 'col'))
- coefficients: float32 [3, 64, 64], replicated
Inputs may be any that keep to these rules, and one draw needn't show every extreme that they name: coarse_kernel equals its transpose. pair_weight equals its transpose.
All inputs are finite; a program needn't handle non-finite values.
Results may differ from a plain program's by a relative error of at most 0.0085.
Values may be sent and summed in bfloat16 or wider, within the bound.
A program may use at most 64 MiB of HBM per device.

v0:
```python
import functools

import jax
import jax.numpy as jnp
from jax import lax
from jax.sharding import Mesh
from jax.sharding import PartitionSpec as P

ROW = ("row_0", "row_1")
COL = ("col_0", "col_1", "col_2")
ROW_COL = ("row_0", "row_1", "col_0", "col_1", "col_2")


def sent_to_all(array, axis):
    copies = jnp.broadcast_to(array, (lax.axis_size(axis), *array.shape))
    return lax.all_to_all(copies, axis, split_axis=0, concat_axis=0, tiled=True)


def joined_along(blocks, dim):
    blocks = jnp.moveaxis(blocks, 0, dim)
    dims = blocks.shape
    return blocks.reshape(*dims[:dim], dims[dim] * dims[dim + 1], *dims[dim + 2 :])


def collect(array, axis, dim):
    blocks = sent_to_all(array, axis)
    return joined_along(blocks, dim)


def split_up(array, dim, count):
    dims = array.shape
    blocks = array.reshape(*dims[:dim], count, dims[dim] // count, *dims[dim + 1 :])
    return jnp.moveaxis(blocks, dim, 0)


def summed_on_arrival(array, axis, dim):
    count = lax.axis_size(axis)
    blocks = lax.all_to_all(split_up(array, dim, count), axis, 0, 0, tiled=True)
    return jnp.sum(blocks, axis=0)


def over_axes(array, axes):
    return functools.reduce(lax.psum, axes, array)


def build_tile(row_correlation, row_neighbor, column_correlation, column_neighbor, coarse, weights):
    band_size = row_correlation.shape[1]
    coarse_count = coarse.shape[0] // band_size
    blocks = coarse.reshape(coarse_count, band_size, coarse_count, band_size)[
        :, :, column_neighbor, :
    ]
    mapped = jnp.einsum(
        "cakb,kbe->cake", blocks, column_correlation, preferred_element_type=jnp.float32
    ).astype(jnp.bfloat16)
    chosen = mapped[row_neighbor]
    product = jnp.einsum(
        "kai,kaje->kije", row_correlation, chosen, preferred_element_type=jnp.float32
    )
    scaled = (product * weights[:, None, :, None]).astype(jnp.bfloat16)
    return scaled.reshape(
        row_correlation.shape[0] * band_size, column_correlation.shape[0] * band_size
    )


def apply_down(kernel_tile, vectors):
    partial_value = jnp.dot(
        kernel_tile, collect(vectors, ROW, 0), preferred_element_type=jnp.float32
    )
    return summed_on_arrival(partial_value, COL, 0)


def on_device(coarse_kernel, correlations, neighbor, pair_weight, energies, start_block):
    row_correlation, row_neighbor = (collect(correlations, COL, 0), collect(neighbor, COL, 0))
    column_correlation, column_neighbor = (collect(correlations, ROW, 0), collect(neighbor, ROW, 0))
    coarse_strip = collect(coarse_kernel, ROW, 0)
    coarse = lax.all_gather(coarse_strip, COL, axis=1, tiled=True)
    row_count = lax.axis_size(ROW)
    col_count = lax.axis_size(COL)
    fine_rows = pair_weight.shape[0]
    per_device = fine_rows // col_count
    weight_grid = pair_weight.reshape(fine_rows, row_count, col_count, per_device)
    weights = lax.dynamic_index_in_dim(weight_grid, lax.axis_index(COL), 2, keepdims=False)
    weights = weights.reshape(fine_rows, row_count * per_device)
    kernel_tile = build_tile(
        row_correlation, row_neighbor, column_correlation, column_neighbor, coarse, weights
    )
    total_rows = float(start_block.shape[0] * row_count * col_count)
    first_gram = over_axes(jnp.dot(start_block.T, start_block), ROW_COL) / total_rows
    lower_first = jnp.linalg.cholesky(first_gram)
    basis = jax.scipy.linalg.solve_triangular(lower_first, start_block.T, lower=True).T
    first_vectors = basis.astype(jnp.bfloat16)
    first_term = apply_down(kernel_tile, first_vectors)
    image = energies[:, None] * basis + first_term
    local_projection = jnp.dot(basis.T, image)
    summed_projection, summed_square = (
        over_axes(local_projection, ROW_COL),
        over_axes(jnp.dot(image.T, image), ROW_COL),
    )
    alpha_first = summed_projection / total_rows
    remainder = image - jnp.dot(basis, alpha_first)
    next_gram = summed_square / total_rows - jnp.dot(alpha_first.T, alpha_first)
    lower_next = jnp.linalg.cholesky(next_gram)
    second = jax.scipy.linalg.solve_triangular(lower_next, remainder.T, lower=True).T
    second_vectors = second.astype(jnp.bfloat16)
    second_term = apply_down(kernel_tile, second_vectors)
    image_next = energies[:, None] * second + second_term - jnp.dot(basis, lower_next)
    alpha_next = over_axes(jnp.dot(second.T, image_next), ROW_COL) / total_rows
    residual = image_next - jnp.dot(second, alpha_next)
    return (residual, jnp.stack([alpha_first, lower_next, alpha_next]))


def solution(mesh):
    split = Mesh(mesh.devices.reshape(8, 2, 2, 4, 2), ("row_0", "row_1", "col_0", "col_1", "col_2"))
    placed = (
        P(ROW, COL),
        P(ROW_COL, None, None),
        P(ROW_COL),
        P(ROW, None),
        P(ROW_COL),
        P(ROW_COL, None),
    )
    return jax.shard_map(
        on_device, mesh=split, in_specs=placed, out_specs=(P(ROW_COL, None), P()), check_vma=False
    )
```

profile of v0, /device:TPU:8, one launch (start us, length us, event | category | flops | bytes accessed | tf_op | source)
XLA Modules:
  0.0 412.5 jit_solution(17453612363734504301)
XLA Ops:
  8.3 21.2 %all_to_all.53 = bf16[16,2,2048]{2,1,0:T(2,128)(2,1)S(1)} all-to-all(bf16[16,2,2048]{2,1,0:T(2,128)(2,1)S(1)} %reshape.132), channel_id=1, replica_groups=mesh['row_0'=8,'row_1'=2,'col_0'=2,'col_1'=4,'col_2'=2] {'row_0','row_1'}, dimensions={0} | all-to-all | bytes 262144 | tf_op jit(solution)/shard_map/all_to_all | solution.py:16
  32.1 5.8 %all-to-all-start.3 = ((s32[16,1,1]{2,1,0:T(1,128)}), s32[16,1,1]{2,1,0:T(1,128)S(1)}, u32[]{:S(2)}, u32[]{:S(2)}) async-start(s32[16,1,1]{2,1,0:T(1,128)} %broadcast_in_dim.12), calls=%async_computation.3 | async-start | bytes 16384 | tf_op jit(solution)/shard_map/all_to_all | solution.py:16
  38.8 27.4 %psum.140 = f32[64,64]{1,0:T(8,128)S(1)} all-reduce(f32[64,64]{1,0:T(8,128)S(1)} %fusion.52), channel_id=1, replica_groups=mesh['row_0'=8,'row_1'=2,'col_0'=2,'col_1'=4,'col_2'=2] {'row_0'}, use_global_device_ids=true, to_apply=%region_0.1 | all-reduce | flops 4096 | bytes 32768 | tf_op jit(solution)/shard_map/psum | solution.py:43
  66.2 9.1 %psum.141 = f32[64,64]{1,0:T(8,128)S(1)} all-reduce(f32[64,64]{1,0:T(8,128)S(1)} %psum.140), channel_id=1, replica_groups=mesh['row_0'=8,'row_1'=2,'col_0'=2,'col_1'=4,'col_2'=2] {'row_1'}, use_global_device_ids=true, to_apply=%region_1.2 | all-reduce | flops 4096 | bytes 32768 | tf_op jit(solution)/shard_map/psum | solution.py:43
  75.3 7.6 %psum.142 = f32[64,64]{1,0:T(8,128)S(1)} all-reduce(f32[64,64]{1,0:T(8,128)S(1)} %psum.141), channel_id=1, replica_groups=mesh['row_0'=8,'row_1'=2,'col_0'=2,'col_1'=4,'col_2'=2] {'col_0'}, use_global_device_ids=true, to_apply=%region_2.3 | all-reduce | flops 4096 | bytes 32768 | tf_op jit(solution)/shard_map/psum | solution.py:43
  82.9 17.4 %psum.143 = f32[64,64]{1,0:T(8,128)S(1)} all-reduce(f32[64,64]{1,0:T(8,128)S(1)} %psum.142), channel_id=1, replica_groups=mesh['row_0'=8,'row_1'=2,'col_0'=2,'col_1'=4,'col_2'=2] {'col_1'}, use_global_device_ids=true, to_apply=%region_3.4 | all-reduce | flops 4096 | bytes 32768 | tf_op jit(solution)/shard_map/psum | solution.py:43
  103.9 5.9 %cholesky.44 = f32[64,64]{1,0:T(8,128)S(1)} custom-call(f32[64,64]{1,0:T(8,128)S(1)} %copy.64), custom_call_target="Cholesky" | custom-call | tf_op jit(solution)/shard_map/jit(cholesky)/cholesky | solution.py:89
  134.1 17.6 %all-to-all-done.2 = bf16[16,1,128,128]{3,2,1,0:T(8,128)(2,1)S(1)} async-done(((bf16[16,1,128,128]{3,2,1,0:T(8,128)(2,1)}), bf16[16,1,128,128]{3,2,1,0:T(8,128)(2,1)S(1)}, u32[]{:S(2)}, u32[]{:S(2)}) %all-to-all-start.2) | async-done | bytes 524320 | tf_op jit(solution)/shard_map/all_to_all | solution.py:16
  151.7 6.0 %all-to-all-start.4 = ((bf16[16,1,128,128]{3,2,1,0:T(8,128)(2,1)}), bf16[16,1,128,128]{3,2,1,0:T(8,128)(2,1)S(1)}, u32[]{:S(2)}, u32[]{:S(2)}) async-start(bf16[16,1,128,128]{3,2,1,0:T(8,128)(2,1)} %broadcast_in_dim.24), calls=%async_computation.4 | async-start | bytes 1048576 | tf_op jit(solution)/shard_map/all_to_all | solution.py:16
  175.8 6.9 %gather_fusion.1 = bf16[16,128,16,128]{3,2,1,0:T(8,128)(2,1)} fusion(bf16[8,128,16,128]{3,2,1,0:T(8,128)(2,1)} %copy.69, s32[1024]{0:T(1024)S(1)} %pad_clamp_fusion), kind=kCustom, calls=%fused_computation.1 | custom fusion | bytes 16777280 | tf_op jit(solution)/shard_map/gather | solution.py:55
  187.0 10.3 %multiply_convert_fusion = bf16[16,16,128,128]{3,2,1,0:T(8,128)(2,1)} fusion(bf16[16,128,16,128]{3,2,1,0:T(8,128)(2,1)} %gather_fusion.1, f32[16,16]{1,0:T(8,128)S(1)} %dynamic-slice_reduce_fusion, bf16[16,1,128,128]{3,2,1,0:T(8,128)(2,1)S(1)} %all-to-all-done.4), kind=kOutput, calls=%fused_computation.2 | convolution fusion | flops 1082130432 | bytes 17302528 | tf_op jit(solution)/shard_map/kai,kaje->kije/dot_general | solution.py:56
  206.5 15.0 %all_to_all.54 = f32[16,128,64]{1,2,0:T(8,128)S(1)} all-to-all(f32[16,128,64]{1,2,0:T(8,128)S(1)} %fusion.12), channel_id=1, replica_groups=mesh['row_0'=8,'row_1'=2,'col_0'=2,'col_1'=4,'col_2'=2] {'col_0','col_1'..., dimensions={0} | all-to-all | bytes 1048576 | tf_op jit(solution)/shard_map/all_to_all | solution.py:38
  221.8 27.7 %all-reduce = (f32[64,64]{1,0:T(8,128)S(1)}, f32[64,64]{1,0:T(8,128)S(1)}) all-reduce(f32[64,64]{1,0:T(8,128)S(1)} %fusion.31, f32[64,64]{1,0:T(8,128)S(1)} %fusion.32), channel_id=1, replica_groups=mesh['row_0'=8,'row_1'=2,'col_0'=2,'col_1'=4,'col_2'=2] {'row_0'}, use_global_device_ids=true, to_apply=%region_13.16 | all-reduce | flops 8192 | bytes 65536 | tf_op jit(solution)/shard_map/psum | solution.py:43
  249.5 10.5 %all-reduce.4 = (f32[64,64]{1,0:T(8,128)S(1)}, f32[64,64]{1,0:T(8,128)S(1)}) all-reduce(f32[64,64]{1,0:T(8,128)S(1)} %get-tuple-element.4, f32[64,64]{1,0:T(8,128)S(1)} %get-tuple-element.5), channel_id=1, replica_groups=mesh['row_0'=8,'row_1'=2,'col_0'=2,'col_1'=4,'col_2'=2] {'row_1'}, use_global_device_ids=true, to_apply=%region_14.17 | all-reduce | flops 8192 | bytes 65536 | tf_op jit(solution)/shard_map/psum | solution.py:43
  260.0 9.3 %all-reduce.3 = (f32[64,64]{1,0:T(8,128)S(1)}, f32[64,64]{1,0:T(8,128)S(1)}) all-reduce(f32[64,64]{1,0:T(8,128)S(1)} %get-tuple-element.12, f32[64,64]{1,0:T(8,128)S(1)} %get-tuple-element.13), channel_id=1, replica_groups=mesh['row_0'=8,'row_1'=2,'col_0'=2,'col_1'=4,'col_2'=2] {'col_0'}, use_global_device_ids=true, to_apply=%region_15.18 | all-reduce | flops 8192 | bytes 65536 | tf_op jit(solution)/shard_map/psum | solution.py:43
  269.3 15.3 %all-reduce.1 = (f32[64,64]{1,0:T(8,128)S(1)}, f32[64,64]{1,0:T(8,128)S(1)}) all-reduce(f32[64,64]{1,0:T(8,128)S(1)} %get-tuple-element.10, f32[64,64]{1,0:T(8,128)S(1)} %get-tuple-element.11), channel_id=1, replica_groups=mesh['row_0'=8,'row_1'=2,'col_0'=2,'col_1'=4,'col_2'=2] {'col_1'}, use_global_device_ids=true, to_apply=%region_16.19 | all-reduce | flops 8192 | bytes 65536 | tf_op jit(solution)/shard_map/psum | solution.py:43
  288.8 5.9 %cholesky.55 = f32[64,64]{1,0:T(8,128)S(1)} custom-call(f32[64,64]{1,0:T(8,128)S(1)} %copy.73), custom_call_target="Cholesky" | custom-call | tf_op jit(solution)/shard_map/jit(cholesky)/cholesky | solution.py:102
  301.2 18.4 %all_to_all.55 = bf16[16,128,64]{1,2,0:T(8,128)(2,1)S(1)} all-to-all(bf16[16,128,64]{1,2,0:T(8,128)(2,1)S(1)} %broadcast_in_dim.26), channel_id=1, replica_groups=mesh['row_0'=8,'row_1'=2,'col_0'=2,'col_1'=4,'col_2'=2] {'row_0','row_1'}, dimensions={0} | all-to-all | bytes 524288 | tf_op jit(solution)/shard_map/all_to_all | solution.py:16
  325.3 5.8 %all-to-all-start.8 = ((f32[16,128,64]{1,2,0:T(8,128)}), f32[16,128,64]{1,2,0:T(8,128)S(1)}, u32[]{:S(2)}, u32[]{:S(2)}) async-start(f32[16,128,64]{1,2,0:T(8,128)} %fusion.9), calls=%async_computation.8 | async-start | bytes 1048576 | tf_op jit(solution)/shard_map/all_to_all | solution.py:38
  331.1 9.5 %all-to-all-done.8 = f32[16,128,64]{1,2,0:T(8,128)S(1)} async-done(((f32[16,128,64]{1,2,0:T(8,128)}), f32[16,128,64]{1,2,0:T(8,128)S(1)}, u32[]{:S(2)}, u32[]{:S(2)}) %all-to-all-start.8) | async-done | bytes 524320 | tf_op jit(solution)/shard_map/all_to_all | solution.py:38
  341.6 27.3 %psum.155 = f32[64,64]{1,0:T(8,128)S(1)} all-reduce(f32[64,64]{1,0:T(8,128)S(1)} %fusion.53), channel_id=1, replica_groups=mesh['row_0'=8,'row_1'=2,'col_0'=2,'col_1'=4,'col_2'=2] {'row_0'}, use_global_device_ids=true, to_apply=%region_19.22 | all-reduce | flops 4096 | bytes 32768 | tf_op jit(solution)/shard_map/psum | solution.py:43
  368.9 8.4 %psum.156 = f32[64,64]{1,0:T(8,128)S(1)} all-reduce(f32[64,64]{1,0:T(8,128)S(1)} %psum.155), channel_id=1, replica_groups=mesh['row_0'=8,'row_1'=2,'col_0'=2,'col_1'=4,'col_2'=2] {'row_1'}, use_global_device_ids=true, to_apply=%region_20.23 | all-reduce | flops 4096 | bytes 32768 | tf_op jit(solution)/shard_map/psum | solution.py:43
  377.3 8.8 %psum.157 = f32[64,64]{1,0:T(8,128)S(1)} all-reduce(f32[64,64]{1,0:T(8,128)S(1)} %psum.156), channel_id=1, replica_groups=mesh['row_0'=8,'row_1'=2,'col_0'=2,'col_1'=4,'col_2'=2] {'col_0'}, use_global_device_ids=true, to_apply=%region_21.24 | all-reduce | flops 4096 | bytes 32768 | tf_op jit(solution)/shard_map/psum | solution.py:43
  386.2 14.6 %psum.158 = f32[64,64]{1,0:T(8,128)S(1)} all-reduce(f32[64,64]{1,0:T(8,128)S(1)} %psum.157), channel_id=1, replica_groups=mesh['row_0'=8,'row_1'=2,'col_0'=2,'col_1'=4,'col_2'=2] {'col_1'}, use_global_device_ids=true, to_apply=%region_22.25 | all-reduce | flops 4096 | bytes 32768 | tf_op jit(solution)/shard_map/psum | solution.py:43
  (74 shorter events, 85.9 us)
Async XLA Ops:
  7.2 31.5 %copy-start = (f32[128,64]{0,1:T(8,128)S(1)}, f32[128,64]{0,1:T(8,128)}, u32[]{:S(2)}) copy-start(f32[128,64]{0,1:T(8,128)} %param.14) | copy-start | bytes 98308
  7.2 150.5 %all-gather.2.cloned.1.call-start = ((), (), s32[]{:S(2)}) async-start(), calls=%async_computation.9 | async-start | bytes 2228224 | tf_op jit(solution)/shard_map/all_gather | solution.py:76
  32.1 79.0 %all-to-all-start.3 = ((s32[16,1,1]{2,1,0:T(1,128)}), s32[16,1,1]{2,1,0:T(1,128)S(1)}, u32[]{:S(2)}, u32[]{:S(2)}) async-start(s32[16,1,1]{2,1,0:T(1,128)} %broadcast_in_dim.12), calls=%async_computation.3 | async-start | bytes 16384 | tf_op jit(solution)/shard_map/all_to_all | solution.py:16
  111.1 15.5 %all-to-all-start.1 = ((s32[16,1,1]{2,1,0:T(1,128)}), s32[16,1,1]{2,1,0:T(1,128)S(1)}, u32[]{:S(2)}, u32[]{:S(2)}) async-start(s32[16,1,1]{2,1,0:T(1,128)} %broadcast_in_dim.12), calls=%async_computation.1 | async-start | bytes 16384 | tf_op jit(solution)/shard_map/all_to_all | solution.py:16
  128.3 23.4 %all-to-all-start.2 = ((bf16[16,1,128,128]{3,2,1,0:T(8,128)(2,1)}), bf16[16,1,128,128]{3,2,1,0:T(8,128)(2,1)S(1)}, u32[]{:S(2)}, u32[]{:S(2)}) async-start(bf16[16,1,128,128]{3,2,1,0:T(8,128)(2,1)} %broadcast_in_dim.24), calls=%async_computation.2 | async-start | bytes 1048576 | tf_op jit(solution)/shard_map/all_to_all | solution.py:16
  151.7 31.0 %all-to-all-start.4 = ((bf16[16,1,128,128]{3,2,1,0:T(8,128)(2,1)}), bf16[16,1,128,128]{3,2,1,0:T(8,128)(2,1)S(1)}, u32[]{:S(2)}, u32[]{:S(2)}) async-start(bf16[16,1,128,128]{3,2,1,0:T(8,128)(2,1)} %broadcast_in_dim.24), calls=%async_computation.4 | async-start | bytes 1048576 | tf_op jit(solution)/shard_map/all_to_all | solution.py:16
  183.5 18.1 %all-to-all-start.5 = ((bf16[16,128,64]{1,2,0:T(8,128)(2,1)}), bf16[16,128,64]{1,2,0:T(8,128)(2,1)S(1)}, u32[]{:S(2)}, u32[]{:S(2)}) async-start(bf16[16,128,64]{1,2,0:T(8,128)(2,1)} %broadcast_in_dim.25), calls=%async_computation.5 | async-start | bytes 524288 | tf_op jit(solution)/shard_map/all_to_all | solution.py:16
  197.3 24.2 %copy-start.1 = (f32[128]{0:T(128)S(1)}, f32[128]{0:T(128)}, u32[]{:S(2)}) copy-start(f32[128]{0:T(128)} %param.13) | copy-start | bytes 1540
  325.3 15.3 %all-to-all-start.8 = ((f32[16,128,64]{1,2,0:T(8,128)}), f32[16,128,64]{1,2,0:T(8,128)S(1)}, u32[]{:S(2)}, u32[]{:S(2)}) async-start(f32[16,128,64]{1,2,0:T(8,128)} %fusion.9), calls=%async_computation.8 | async-start | bytes 1048576 | tf_op jit(solution)/shard_map/all_to_all | solution.py:38
Sparse Core Ops, SparseCore 0:
  31.0 30.9 all-gather.1
where the time goes:
time: 416 us; the launch traced here: 412 us
  blocking collectives  248 us (60%)
  waiting for transfers between devices  36.1 us (9%)
  starting transfers between devices  31.5 us (8%)
  local copies, waits for them, and re-layouts  28.3 us (7%)
  matrix products  27.4 us (7%)
  other arithmetic  25.7 us (6%)
  between operations  15.1 us (4%)
    psum x15, blocking collectives, over_axes(): return functools.reduce(lax.psum, axes, array)  194 us
    all_to_all x2, blocking collectives, sent_to_all(): return lax.all_to_all(copies, axis, split_axis=0, concat_axis=0, tiled=True)  39.6 us
    all_to_all x5, waiting for transfers between devices, sent_to_all(): return lax.all_to_all(copies, axis, split_axis=0, concat_axis=0, tiled=True)  26.6 us
    all_to_all x5, starting transfers between devices, sent_to_all(): return lax.all_to_all(copies, axis, split_axis=0, concat_axis=0, tiled=True)  25.6 us
    all_to_all x1, blocking collectives, summed_on_arrival(): blocks = lax.all_to_all(split_up(array, dim, count), axis, 0, 0, tiled=True)  15 us
    dot_general x2, matrix products, apply_down(): jnp.dot(kernel_tile, collect(vectors, ROW, 0), preferred_element_type=jnp...  10.7 us
    dot_general x1, matrix products, build_tile(): jnp.einsum('kai,kaje->kije', row_correlation, chosen, preferred_element_t...  10.3 us
    all_to_all x1, waiting for transfers between devices, summed_on_arrival(): blocks = lax.all_to_all(split_up(array, dim, count), axis, 0, 0, tiled=True)  9.47 us
  transfers between devices with their start and end apart: 7, of which 4 were waited for; matrix products, arithmetic and copies ran while one was open for 13% of the time, Pallas kernels for 0%

commit v1 on v0

v1 whole, which is shorter than its diff:
```python
import functools

import jax
import jax.numpy as jnp
from jax import lax
from jax.experimental import pallas as pl
from jax.experimental.pallas import tpu as pltpu
from jax.sharding import PartitionSpec as P

MESH = pl.DeviceIdType.MESH
HIGH = lax.Precision.HIGHEST
F32 = jnp.float32
BF16 = jnp.bfloat16
B = 128
M = 64
NX, NY, NZ = 4, 4, 8
NXY = NX * NY
TOTAL = 32768.0


def nn(a, b, precision=HIGH):
    return lax.dot_general(
        a, b, (((1,), (0,)), ((), ())), precision=precision, preferred_element_type=F32
    )


def nt(a, b, precision=HIGH):
    return lax.dot_general(
        a, b, (((1,), (1,)), ((), ())), precision=precision, preferred_element_type=F32
    )


def lanes(shape):
    return lax.broadcasted_iota(jnp.int32, shape, 1)


def rows(shape):
    return lax.broadcasted_iota(jnp.int32, shape, 0)


def packed_product(left, right):
    twice = jnp.concatenate([right, right], axis=0)
    upper = nt(left[: M // 2], twice)
    lower = nt(left[M // 2 :], twice)
    return jnp.where(lanes(upper.shape) < M, upper, lower)


def unpacked(packed):
    return jnp.concatenate([packed, pltpu.roll(packed, M, axis=1)], axis=0)


def factor(gram, out_ref):
    shape = (M, 2 * M)
    start = jnp.where(
        lanes(shape) < M, gram, jnp.where(lanes(shape) - M == rows(shape), 1.0, 0.0)
    )

    def eight(block, matrix):
        done = []
        for s in range(8):
            root = lax.rsqrt(matrix[s : s + 1, s : s + 1])
            row = matrix[s : s + 1, :] * root
            column = matrix[:, s : s + 1] * root
            done.append(row)
            matrix = matrix - column * row
        finished = pltpu.roll(jnp.concatenate(done, axis=0), 8 * block, axis=1)
        out_ref[pl.ds(pl.multiple_of(8 * block, 8), 8), :] = finished
        matrix = jnp.concatenate([matrix[8:], matrix[:8]], axis=0)
        return pltpu.roll(matrix, 2 * M - 8, axis=1)

    lax.fori_loop(0, M // 8, eight, start)
    result = out_ref[...]
    upper = jnp.where(lanes(shape) >= rows(shape), result, 0.0)[:, :M]
    inverse = pltpu.roll(result, M, axis=1)[:, :M]
    return upper, inverse


def kernel(
    coarse_ref, corr_ref, near_ref, weight_ref, energy_ref, start_ref,
    residual_ref, coef_ref,
    cbuf, chalf, near_k, near_own, near_xy, near_z, near_xy_s, near_z_s, w_other, w_s,
    gk, gxy, gz, gsend, fac,
    ubuf, tbuf, ypart, ysend, yk, rsend, rbuf,
    ak, asend, az, axy, afull, hk, hxy, hz, hsend,
    send, recv, local,
):
    row, col = lax.axis_index("row"), lax.axis_index("col")
    z, yh = row // 2, row % 2
    yl, x, k = col // 8, (col // 2) % 4, col % 2
    y = yh * 2 + yl
    me_xy = y * NX + x

    def device(x_, y_, z_, k_):
        return (z_ * 2 + y_ // 2, (y_ % 2) * 8 + x_ * 2 + k_)

    sibling = device(x, y, z, 1 - k)
    x_ring = [device((x + d) % NX, y, z, k) for d in range(1, NX)]
    y_ring = [device(x, (y + d) % NY, z, k) for d in range(1, NY)]
    z_ring = [device(x, y, (z + d) % NZ, k) for d in range(1, NZ)]
    plane = [
        device((x + dx) % NX, (y + dy) % NY, z, k)
        for dy in range(NY)
        for dx in range(NX)
        if dx or dy
    ]
    count = [0]
    sent = []

    def push(src, dst, targets, like=None):
        i = count[0]
        count[0] += 1
        for target in targets:
            pltpu.make_async_remote_copy(
                src_ref=src, dst_ref=dst, send_sem=send.at[i], recv_sem=recv.at[i],
                device_id=target, device_id_type=MESH,
            ).start()
        like = dst if like is None else like
        sent.append((i, like))

        def wait():
            pltpu.make_async_copy(like, like, recv.at[i]).wait()

        return wait

    barrier = pltpu.get_barrier_semaphore()
    partners = [sibling] + plane + z_ring
    for target in partners:
        pl.semaphore_signal(barrier, inc=1, device_id=target, device_id_type=MESH)
    near_own[...] = jnp.full((8, B), near_ref[0], jnp.int32)
    start_t = start_ref[...].T
    gk[0] = packed_product(start_t, start_t)
    pl.semaphore_wait(barrier, len(partners))

    other_half = pl.ds(pl.multiple_of((1 - k) * 32, 32), 32)
    own_half = pl.ds(pl.multiple_of(k * 32, 32), 32)
    got_half = push(coarse_ref.at[other_half], chalf, [sibling])
    got_gk = push(gk.at[0], gk.at[1], [sibling])
    got_near_k = push(near_own, near_k, [sibling])

    got_half()
    shape = (M, B)
    place_own = jnp.where(lanes(shape) == rows(shape) + M * k, 1.0, 0.0).astype(BF16)
    place_sib = jnp.where(lanes(shape) == rows(shape) + M * (1 - k), 1.0, 0.0).astype(BF16)
    strip = nn(coarse_ref[own_half, :], place_own, None) + nn(chalf[...], place_sib, None)
    cbuf[z, yl, x, yh, k] = strip.astype(BF16)
    mine = cbuf.at[z, yl, x, yh, k]
    got_a = push(mine, mine, z_ring, cbuf.at[pl.ds(0, 7), 0, 0, 0, 0])

    got_gk()
    gxy[me_xy] = gk[0] + gk[1]
    got_gxy = push(gxy.at[me_xy], gxy.at[me_xy], plane, gxy.at[pl.ds(0, NXY - 1)])
    got_w = push(weight_ref, w_other, [y_ring[1]])
    near_xy[me_xy] = near_own[...]
    got_near_xy = push(near_xy.at[me_xy], near_xy.at[me_xy], plane, near_xy.at[pl.ds(0, NXY - 1)])
    got_near_k()
    near_z[z] = jnp.where(rows((8, B)) == 0, near_own[...], near_k[...])
    got_near_z = push(near_z.at[z], near_z.at[z], z_ring, near_z.at[pl.ds(0, NZ - 1)])

    got_a()
    b_first = cbuf.at[pl.ds(0, 4), yl, x, yh, k]
    b_second = cbuf.at[pl.ds(4, 4), yl, x, yh, k]
    twelve = cbuf.at[pl.ds(0, 6), :, 0, 0, 0]
    got_b1 = push(b_first, b_first, x_ring, twelve)
    got_b2 = push(b_second, b_second, y_ring, twelve)

    got_gxy()
    gz[z] = jnp.sum(gxy[...], axis=0)
    got_gz = push(gz.at[z], gz.at[z], z_ring, gz.at[pl.ds(0, NZ - 1)])

    got_b1()
    c_first = cbuf.at[pl.ds(0, 4), yl, :, yh, k]
    c_second = cbuf.at[pl.ds(4, 4), :, x, :, k]
    fortyeight = cbuf.at[pl.ds(0, 6), :, :, 0, 0]
    got_c1 = push(c_first, c_first, y_ring, fortyeight)
    got_b2()
    got_c2 = push(c_second, c_second, x_ring, fortyeight)

    got_w()
    got_near_xy()
    got_near_z()
    locals_ = [
        pltpu.make_async_copy(weight_ref, w_s.at[yh], local.at[0]),
        pltpu.make_async_copy(w_other, w_s.at[1 - yh], local.at[1]),
        pltpu.make_async_copy(near_xy, near_xy_s, local.at[2]),
        pltpu.make_async_copy(near_z, near_z_s, local.at[3]),
    ]
    for c in locals_:
        c.start()

    corr = corr_ref[0].astype(F32)

    got_gz()
    gram = unpacked(jnp.sum(gz[...], axis=0) * (1.0 / TOTAL))
    _, inverse0 = factor(gram, fac.at[0])
    basis = nn(inverse0, start_t)

    def gather(step, vectors):
        ubuf[step, me_xy] = nt(vectors, corr).astype(BF16)
        mine_ = ubuf.at[step, me_xy]
        return push(mine_, mine_, plane, ubuf.at[step, pl.ds(0, NXY - 1)])

    got_u = gather(0, basis)
    for c in locals_:
        c.wait()
    got_c1()
    got_c2()
    half_all = cbuf.at[:, :, :, :, k]
    got_d = push(half_all, half_all, [sibling])
    got_d()
    got_u()

    def apply(step):
        def one_source(q, _):
            block = cbuf[near_xy_s[q, 0, 0]].reshape(8, B, B)
            vector = ubuf[step, q]
            for c in range(8):
                tbuf[q, c] = nn(vector, block[c], None)
            return 0

        lax.fori_loop(0, NXY, one_source, 0)

        def target(z_, other, out):
            near = near_z_s[z_, other, 0]
            kk = jnp.where(other == 1, 1 - k, k) if not isinstance(other, int) else (1 - k if other else k)
            place = z_ * 32 + yh * 16 + yl * 8 + x * 2 + kk
            total = jnp.zeros((M, B), F32)
            for q in range(NXY):
                qy, qx = q // NX, q % NX
                w = w_s[qy // 2, (qy % 2) * 8 + qx * 2 + k, place]
                total = total + w * tbuf[q, near]
            out[z_] = total

        def for_sibling(z_, _):
            target(z_, 1, ysend.at[step])
            return 0

        def for_own(z_, _):
            target(z_, 0, ypart)
            return 0

        lax.fori_loop(0, NZ, for_sibling, 0)
        got_yk = push(ysend.at[step], yk.at[step], [sibling])
        lax.fori_loop(0, NZ, for_own, 0)
        got_yk()
        total = ypart[...] + yk[step]
        rsend[step] = total.astype(BF16)
        i = count[0]
        count[0] += 1
        for d in range(1, NZ):
            there = (z + d) % NZ
            pltpu.make_async_remote_copy(
                src_ref=rsend.at[step, there], dst_ref=rbuf.at[step, z],
                send_sem=send.at[i], recv_sem=recv.at[i],
                device_id=z_ring[d - 1], device_id_type=MESH,
            ).start()
        like = rbuf.at[step, pl.ds(0, NZ - 1)]
        sent.append((i, like))
        rbuf[step, z] = jnp.zeros((M, B), BF16)
        own = ypart[z] + yk[step, z]

        def result():
            pltpu.make_async_copy(like, like, recv.at[i]).wait()
            summed = own + jnp.sum(rbuf[step].astype(F32), axis=0)
            return nn(summed, corr)

        return result

    energy = energy_ref[...]
    image = energy * basis + apply(0)()

    got_u = gather(1, image)
    ak[0] = nt(image, jnp.concatenate([basis, image], axis=0))
    got_ak = push(ak.at[0], ak.at[1], [sibling])
    got_ak()
    asend[...] = (ak[0] + ak[1]).reshape(NZ, 8, B)
    az[z] = asend[z]
    i_az = count[0]
    count[0] += 1
    for d in range(1, NZ):
        there = (z + d) % NZ
        pltpu.make_async_remote_copy(
            src_ref=asend.at[there], dst_ref=az.at[z], send_sem=send.at[i_az], recv_sem=recv.at[i_az],
            device_id=z_ring[d - 1], device_id_type=MESH,
        ).start()
    like_az = az.at[pl.ds(0, NZ - 1)]
    sent.append((i_az, like_az))

    got_u()
    second_sum = apply_started = None
    pltpu.make_async_copy(like_az, like_az, recv.at[i_az]).wait()
    axy[me_xy] = jnp.sum(az[...], axis=0)
    got_axy = push(axy.at[me_xy], axy.at[me_xy], plane, axy.at[pl.ds(0, NXY - 1)])
    second_sum = apply(1)
    got_axy()
    afull[z] = jnp.sum(axy[...], axis=0)
    got_afull = push(afull.at[z], afull.at[z], z_ring, afull.at[pl.ds(0, NZ - 1)])
    got_afull()
    both = afull[...].reshape(M, B) * (1.0 / TOTAL)
    alpha_t = both[:, :M]
    next_gram = pltpu.roll(both, M, axis=1)[:, :M] - nt(alpha_t, alpha_t)
    next_gram = jnp.concatenate([next_gram, next_gram], axis=1)
    upper1, inverse1 = factor(next_gram, fac.at[1])
    second = nn(inverse1, image - nn(alpha_t, basis))
    minus = nn(upper1, basis)
    less = energy * image - nn(alpha_t, image)
    image_next = nn(inverse1, less + second_sum()) - minus

    hsend[...] = packed_product(image_next, second)
    got_hk = push(hsend, hk, [sibling])
    got_hk()
    hxy[me_xy] = hsend[...] + hk[...]
    got_hxy = push(hxy.at[me_xy], hxy.at[me_xy], plane, hxy.at[pl.ds(0, NXY - 1)])
    got_hxy()
    hz[z] = jnp.sum(hxy[...], axis=0)
    got_hz = push(hz.at[z], hz.at[z], z_ring, hz.at[pl.ds(0, NZ - 1)])
    coef_ref[0] = alpha_t
    coef_ref[1] = upper1
    got_hz()
    alpha_next_t = unpacked(jnp.sum(hz[...], axis=0) * (1.0 / TOTAL))[:, :M]
    coef_ref[2] = alpha_next_t
    residual_ref[...] = image_next - nn(alpha_next_t, second)

    for i, like in sent:
        pltpu.make_async_copy(like, like, send.at[i]).wait()


def on_device(coarse_kernel, correlations, neighbor, pair_weight, energies, start_block):
    vmem = pl.BlockSpec(memory_space=pltpu.VMEM)
    smem = pl.BlockSpec(memory_space=pltpu.SMEM)
    residual_t, coefficients_t = pl.pallas_call(
        kernel,
        out_shape=(
            jax.ShapeDtypeStruct((M, B), F32),
            jax.ShapeDtypeStruct((3, M, M), F32),
        ),
        in_specs=[vmem, vmem, smem, vmem, vmem, vmem],
        out_specs=(vmem, vmem),
        scratch_shapes=[
            pltpu.VMEM((8, 2, 4, 2, 2, 32, B), BF16),
            pltpu.VMEM((32, M), BF16),
            pltpu.VMEM((8, B), jnp.int32),
            pltpu.VMEM((8, B), jnp.int32),
            pltpu.VMEM((NXY, 8, B), jnp.int32),
            pltpu.VMEM((NZ, 8, B), jnp.int32),
            pltpu.SMEM((NXY, 8, B), jnp.int32),
            pltpu.SMEM((NZ, 8, B), jnp.int32),
            pltpu.VMEM((16, 256), F32),
            pltpu.SMEM((2, 16, 256), F32),
            pltpu.VMEM((2, M // 2, B), F32),
            pltpu.VMEM((NXY, M // 2, B), F32),
            pltpu.VMEM((NZ, M // 2, B), F32),
            pltpu.VMEM((M // 2, B), F32),
            pltpu.VMEM((2, M, B), F32),
            pltpu.VMEM((2, NXY, M, B), BF16),
            pltpu.VMEM((NXY, 8, M, B), F32),
            pltpu.VMEM((NZ, M, B), F32),
            pltpu.VMEM((2, NZ, M, B), F32),
            pltpu.VMEM((2, NZ, M, B), F32),
            pltpu.VMEM((2, NZ, M, B), BF16),
            pltpu.VMEM((2, NZ, M, B), BF16),
            pltpu.VMEM((2, M, B), F32),
            pltpu.VMEM((NZ, 8, B), F32),
            pltpu.VMEM((NZ, 8, B), F32),
            pltpu.VMEM((NXY, 8, B), F32),
            pltpu.VMEM((NZ, 8, B), F32),
            pltpu.VMEM((M // 2, B), F32),
            pltpu.VMEM((NXY, M // 2, B), F32),
            pltpu.VMEM((NZ, M // 2, B), F32),
            pltpu.VMEM((M // 2, B), F32),
            pltpu.SemaphoreType.DMA((32,)),
            pltpu.SemaphoreType.DMA((32,)),
            pltpu.SemaphoreType.DMA((4,)),
        ],
        compiler_params=pltpu.CompilerParams(
            collective_id=0, has_side_effects=True, vmem_limit_bytes=40 << 20
        ),
    )(coarse_kernel, correlations, neighbor, pair_weight, energies.reshape(1, B), start_block)
    return residual_t.T, jnp.swapaxes(coefficients_t, 1, 2)


def solution(mesh):
    both = ("row", "col")
    return jax.shard_map(
        on_device,
        mesh=mesh,
        in_specs=(
            P("row", "col"),
            P(both, None, None),
            P(both),
            P("row", None),
            P(both),
            P(both, None),
        ),
        out_specs=(P(both, None), P()),
        check_vma=False,
    )
```

time: 416 us -> 90.1 us (0.22)
  blocking collectives: 248 us -> 0 us
  Pallas kernels: 0 us -> 86 us
  waiting for transfers between devices: 36.1 us -> 0 us
  starting transfers between devices: 31.5 us -> 0 us
  matrix products: 27.4 us -> 0 us
  local copies, waits for them, and re-layouts: 28.3 us -> 2.24 us
  other arithmetic: 25.7 us -> 0 us
  between operations: 15.1 us -> 1.35 us
    psum x15 -> x0, blocking collectives: 194 us -> none  [over_axes(): return functools.reduce(lax.psum, axes, array)]
    pallas_call x0 -> x1, Pallas kernels: none -> 86 us  [on_device(): pl.pallas_call(kernel, out_shape=(jax.ShapeDtypeStruct((M, B), F32), jax....]
    all_to_all x3 -> x0, blocking collectives: 54.6 us -> none  [the longest x2 39.6 us: sent_to_all(): return lax.all_to_all(copies, axis, split_axis=0, concat_axis=0, tiled=True)]
    all_to_all x6 -> x0, waiting for transfers between devices: 36.1 us -> none  [the longest x5 26.6 us: sent_to_all(): return lax.all_to_all(copies, axis, split_axis=0, concat_axis=0, tiled=True)]
    all_to_all x6 -> x0, starting transfers between devices: 31.4 us -> none  [the longest x5 25.6 us: sent_to_all(): return lax.all_to_all(copies, axis, split_axis=0, concat_axis=0, tiled=True)]
    dot_general x12 -> x0, matrix products: 26.9 us -> none  [the longest x2 10.7 us: apply_down(): jnp.dot(kernel_tile, collect(vectors, ROW, 0), preferred_element_type=jnp...]
    another operation x13 -> x0, other arithmetic: 24.8 us -> none  [the longest x3 6.53 us: on_device(): lower_first = jnp.linalg.cholesky(first_gram)]
    gather x2 -> x0, local copies, waits for them, and re-layouts: 9.92 us -> none  [the longest x1 6.91 us: build_tile(): chosen = mapped[row_neighbor]]
  transfers between devices with their start and end apart: 7 -> 0, of which waited for: 4 -> 0; matrix products, arithmetic and copies ran while one was open for 13% -> 0% of each run, Pallas kernels for 0% -> 0%
where the time goes in v1:
time: 90.1 us; the launch traced here: 89.6 us
  Pallas kernels  86 us (95%)
  local copies, waits for them, and re-layouts  2.24 us (2%)
  between operations  1.35 us (1%)
    pallas_call x1, Pallas kernels, on_device(): pl.pallas_call(kernel, out_shape=(jax.ShapeDtypeStruct((M, B), F32), jax....  86 us
    unnamed x11, local copies, waits for them, and re-layouts  2.24 us

profile of v1, /device:TPU:8, one launch (start us, length us, event | category | flops | bytes accessed | tf_op | source)
XLA Modules:
  0.0 89.6 jit_solution(12797960862713959147)
XLA Ops:
  1.3 0.0 copy-start
  1.3 0.0 copy-start.1
  1.3 0.0 copy-start.2
  1.3 0.0 copy-start.3
  1.3 0.9 copy.8.start_ref
  2.2 0.0 copy-done
  2.2 0.0 copy-done.1
  2.2 0.0 copy-done.2
  2.2 0.0 copy-done.3
  2.2 86.0 %shard_map.77 = (f32[64,128]{1,0:T(8,128)S(1)}, f32[3,64,64]{2,1,0:T(8,128)S(1)}) custom-call(bf16[64,64]{1,0:T(8,128)(2,1)S(1)} %copy-done.1, bf16[1,128,128]{2,1,0:T(8,128)(2,1)S(1)} %copy-done, s32[1]{0:T(128)S(6)} %copy.11.near_ref, f32[16,256]{1,0:T(8,128)S(1)} %copy-done.2, f32[1,128]{1,0:T(1,128)S(1)} %bitcast.5, f32[128,64]{1,0:T(8,128)S(1)} %copy.8.start_ref), custom_call_target="tpu_custom_call" | custom-call | tf_op jit(solution)/shard_map/pallas_call | solution.py:330
  88.2 0.7 copy.9
  89.0 0.6 copy.12
Async XLA Ops:
  1.3 0.9 %copy-start = (bf16[1,128,128]{2,1,0:T(8,128)(2,1)S(1)}, bf16[1,128,128]{2,1,0:T(8,128)(2,1)}, u32[]{:S(2)}) copy-start(bf16[1,128,128]{2,1,0:T(8,128)(2,1)} %corr_ref.1) | copy-start | bytes 98308
  1.3 0.9 %copy-start.1 = (bf16[64,64]{1,0:T(8,128)(2,1)S(1)}, bf16[64,64]{1,0:T(8,128)(2,1)}, u32[]{:S(2)}) copy-start(bf16[64,64]{1,0:T(8,128)(2,1)} %coarse_ref.1) | copy-start | bytes 24580
  1.3 0.9 %copy-start.2 = (f32[16,256]{1,0:T(8,128)S(1)}, f32[16,256]{1,0:T(8,128)}, u32[]{:S(2)}) copy-start(f32[16,256]{1,0:T(8,128)} %weight_ref.1) | copy-start | bytes 49156
  1.3 0.9 %copy-start.3 = (f32[128]{0:T(128)S(1)}, f32[128]{0:T(128)}, u32[]{:S(2)}) copy-start(f32[128]{0:T(128)} %param.10) | copy-start | bytes 1540

commit v2 on v1

--- a/solution.py
+++ b/solution.py
@@ -55,15 +55,42 @@
         lanes(shape) < M, gram, jnp.where(lanes(shape) - M == rows(shape), 1.0, 0.0)
     )
 
+    def four(matrix, s):
+        c = [jnp.broadcast_to(matrix[:, s + i : s + i + 1], shape) for i in range(4)]
+        r = [matrix[s + i : s + i + 1, :] for i in range(4)]
+        p = [[c[j][s + i : s + i + 1, :] for j in range(4)] for i in range(4)]
+
+        def pair(i):
+            first, cross, last = p[i][i], p[i][i + 1], p[i + 1][i + 1]
+            det = first * last - cross * cross
+            root = lax.rsqrt(det)
+            inverse = root * root
+            scale = lax.rsqrt(first)
+            upper = r[i] * scale
+            lower = (r[i + 1] - r[i] * (cross * scale * scale)) * (root * first * scale)
+            return last * inverse, -cross * inverse, first * inverse, [upper, lower]
+
+        i00, i01, i11, done = pair(0)
+        for i in (2, 3):
+            w0 = p[0][i] * i00 + p[1][i] * i01
+            w1 = p[0][i] * i01 + p[1][i] * i11
+            r[i] = r[i] - w0 * r[0] - w1 * r[1]
+            c[i] = c[i] - w0 * c[0] - w1 * c[1]
+            for j in range(i, 4):
+                p[i][j] = p[i][j] - w0 * p[0][j] - w1 * p[1][j]
+        j00, j01, j11, more = pair(2)
+        matrix = matrix - (
+            c[0] * (i00 * r[0] + i01 * r[1])
+            + c[1] * (i01 * r[0] + i11 * r[1])
+            + c[2] * (j00 * r[2] + j01 * r[3])
+            + c[3] * (j01 * r[2] + j11 * r[3])
+        )
+        return matrix, done + more
+
     def eight(block, matrix):
-        done = []
-        for s in range(8):
-            root = lax.rsqrt(matrix[s : s + 1, s : s + 1])
-            row = matrix[s : s + 1, :] * root
-            column = matrix[:, s : s + 1] * root
-            done.append(row)
-            matrix = matrix - column * row
-        finished = pltpu.roll(jnp.concatenate(done, axis=0), 8 * block, axis=1)
+        matrix, done = four(matrix, 0)
+        matrix, more = four(matrix, 4)
+        finished = pltpu.roll(jnp.concatenate(done + more, axis=0), 8 * block, axis=1)
         out_ref[pl.ds(pl.multiple_of(8 * block, 8), 8), :] = finished
         matrix = jnp.concatenate([matrix[8:], matrix[:8]], axis=0)
         return pltpu.roll(matrix, 2 * M - 8, axis=1)
@@ -81,7 +108,7 @@
     cbuf, chalf, near_k, near_own, near_xy, near_z, near_xy_s, near_z_s, w_other, w_s,
     gk, gxy, gz, gsend, fac,
     ubuf, tbuf, ypart, ysend, yk, rsend, rbuf,
-    ak, asend, az, axy, afull, hk, hxy, hz, hsend,
+    uz, ak, asend, az, axy, afull, hk, hxy, hz, hsend,
     send, recv, local,
 ):
     row, col = lax.axis_index("row"), lax.axis_index("col")
@@ -105,13 +132,15 @@
     ]
     count = [0]
     sent = []
+    pending = []
 
     def push(src, dst, targets, like=None):
         i = count[0]
         count[0] += 1
-        for target in targets:
+        for d, target in enumerate(targets):
             pltpu.make_async_remote_copy(
-                src_ref=src, dst_ref=dst, send_sem=send.at[i], recv_sem=recv.at[i],
+                src_ref=src(d) if callable(src) else src, dst_ref=dst,
+                send_sem=send.at[i], recv_sem=recv.at[i],
                 device_id=target, device_id_type=MESH,
             ).start()
         like = dst if like is None else like
@@ -119,7 +148,9 @@
 
         def wait():
             pltpu.make_async_copy(like, like, recv.at[i]).wait()
-
+            pending.remove(wait)
+
+        pending.append(wait)
         return wait
 
     barrier = pltpu.get_barrier_semaphore()
@@ -127,7 +158,7 @@
     for target in partners:
         pl.semaphore_signal(barrier, inc=1, device_id=target, device_id_type=MESH)
     near_own[...] = jnp.full((8, B), near_ref[0], jnp.int32)
-    start_t = start_ref[...].T
+    start_t = start_ref[...]
     gk[0] = packed_product(start_t, start_t)
     pl.semaphore_wait(barrier, len(partners))
 
@@ -186,6 +217,7 @@
     ]
     for c in locals_:
         c.start()
+        pending.append(c.wait)
 
     corr = corr_ref[0].astype(F32)
 
@@ -202,6 +234,7 @@
     got_u = gather(0, basis)
     for c in locals_:
         c.wait()
+        pending.remove(c.wait)
     got_c1()
     got_c2()
     half_all = cbuf.at[:, :, :, :, k]
@@ -217,12 +250,11 @@
                 tbuf[q, c] = nn(vector, block[c], None)
             return 0
 
-        lax.fori_loop(0, NXY, one_source, 0)
+        lax.fori_loop(0, NXY, one_source, 0, unroll=4)
 
         def target(z_, other, out):
             near = near_z_s[z_, other, 0]
-            kk = jnp.where(other == 1, 1 - k, k) if not isinstance(other, int) else (1 - k if other else k)
-            place = z_ * 32 + yh * 16 + yl * 8 + x * 2 + kk
+            place = z_ * 32 + yh * 16 + yl * 8 + x * 2 + (1 - k if other else k)
             total = jnp.zeros((M, B), F32)
             for q in range(NXY):
                 qy, qx = q // NX, q % NX
@@ -244,22 +276,15 @@
         got_yk()
         total = ypart[...] + yk[step]
         rsend[step] = total.astype(BF16)
-        i = count[0]
-        count[0] += 1
-        for d in range(1, NZ):
-            there = (z + d) % NZ
-            pltpu.make_async_remote_copy(
-                src_ref=rsend.at[step, there], dst_ref=rbuf.at[step, z],
-                send_sem=send.at[i], recv_sem=recv.at[i],
-                device_id=z_ring[d - 1], device_id_type=MESH,
-            ).start()
-        like = rbuf.at[step, pl.ds(0, NZ - 1)]
-        sent.append((i, like))
+        got_r = push(
+            lambda d: rsend.at[step, (z + d + 1) % NZ], rbuf.at[step, z], z_ring,
+            rbuf.at[step, pl.ds(0, NZ - 1)],
+        )
         rbuf[step, z] = jnp.zeros((M, B), BF16)
         own = ypart[z] + yk[step, z]
 
         def result():
-            pltpu.make_async_copy(like, like, recv.at[i]).wait()
+            got_r()
             summed = own + jnp.sum(rbuf[step].astype(F32), axis=0)
             return nn(summed, corr)
 
@@ -269,54 +294,60 @@
     image = energy * basis + apply(0)()
 
     got_u = gather(1, image)
+    uz[z] = ubuf[1, me_xy]
+    got_uz = push(uz.at[z], uz.at[z], z_ring, uz.at[pl.ds(0, NZ - 1)])
     ak[0] = nt(image, jnp.concatenate([basis, image], axis=0))
     got_ak = push(ak.at[0], ak.at[1], [sibling])
+    energy_product = packed_product(image, energy * image)
     got_ak()
     asend[...] = (ak[0] + ak[1]).reshape(NZ, 8, B)
     az[z] = asend[z]
-    i_az = count[0]
-    count[0] += 1
-    for d in range(1, NZ):
-        there = (z + d) % NZ
-        pltpu.make_async_remote_copy(
-            src_ref=asend.at[there], dst_ref=az.at[z], send_sem=send.at[i_az], recv_sem=recv.at[i_az],
-            device_id=z_ring[d - 1], device_id_type=MESH,
-        ).start()
-    like_az = az.at[pl.ds(0, NZ - 1)]
-    sent.append((i_az, like_az))
-
-    got_u()
-    second_sum = apply_started = None
-    pltpu.make_async_copy(like_az, like_az, recv.at[i_az]).wait()
+    got_az = push(
+        lambda d: asend.at[(z + d + 1) % NZ], az.at[z], z_ring, az.at[pl.ds(0, NZ - 1)]
+    )
+
+    got_az()
     axy[me_xy] = jnp.sum(az[...], axis=0)
     got_axy = push(axy.at[me_xy], axy.at[me_xy], plane, axy.at[pl.ds(0, NXY - 1)])
+    got_u()
     second_sum = apply(1)
+
+    got_uz()
+    upper = jnp.zeros((M // 2, B), F32)
+    lower = upper
+    for d in range(NZ):
+        twice = jnp.concatenate([rsend[1, d], rsend[1, d]], axis=0)
+        vector = uz[d]
+        upper = upper + nt(vector[: M // 2], twice, None)
+        lower = lower + nt(vector[M // 2 :], twice, None)
+    hsend[...] = energy_product + jnp.where(lanes(upper.shape) < M, upper, lower)
+    got_hk = push(hsend, hk, [sibling])
     got_axy()
     afull[z] = jnp.sum(axy[...], axis=0)
     got_afull = push(afull.at[z], afull.at[z], z_ring, afull.at[pl.ds(0, NZ - 1)])
+    got_hk()
+    hxy[me_xy] = hsend[...] + hk[...]
+    got_hxy = push(hxy.at[me_xy], hxy.at[me_xy], plane, hxy.at[pl.ds(0, NXY - 1)])
+    image_sum = energy * image + second_sum()
+    got_hxy()
+    hz[z] = jnp.sum(hxy[...], axis=0)
+    got_hz = push(hz.at[z], hz.at[z], z_ring, hz.at[pl.ds(0, NZ - 1)])
     got_afull()
     both = afull[...].reshape(M, B) * (1.0 / TOTAL)
     alpha_t = both[:, :M]
-    next_gram = pltpu.roll(both, M, axis=1)[:, :M] - nt(alpha_t, alpha_t)
-    next_gram = jnp.concatenate([next_gram, next_gram], axis=1)
-    upper1, inverse1 = factor(next_gram, fac.at[1])
+    square = pltpu.roll(both, M, axis=1)[:, :M]
+    next_gram = square - nt(alpha_t, alpha_t)
+    upper1, inverse1 = factor(jnp.concatenate([next_gram, next_gram], axis=1), fac.at[1])
     second = nn(inverse1, image - nn(alpha_t, basis))
-    minus = nn(upper1, basis)
-    less = energy * image - nn(alpha_t, image)
-    image_next = nn(inverse1, less + second_sum()) - minus
-
-    hsend[...] = packed_product(image_next, second)
-    got_hk = push(hsend, hk, [sibling])
-    got_hk()
-    hxy[me_xy] = hsend[...] + hk[...]
-    got_hxy = push(hxy.at[me_xy], hxy.at[me_xy], plane, hxy.at[pl.ds(0, NXY - 1)])
-    got_hxy()
-    hz[z] = jnp.sum(hxy[...], axis=0)
-    got_hz = push(hz.at[z], hz.at[z], z_ring, hz.at[pl.ds(0, NZ - 1)])
+    image_next = nn(inverse1, image_sum - nn(alpha_t, image)) - nn(upper1, basis)
+    known = (
+        nt(alpha_t, nn(alpha_t, alpha_t)) - nn(alpha_t, square) - nt(square, alpha_t)
+    )
     coef_ref[0] = alpha_t
     coef_ref[1] = upper1
     got_hz()
-    alpha_next_t = unpacked(jnp.sum(hz[...], axis=0) * (1.0 / TOTAL))[:, :M]
+    middle = unpacked(jnp.sum(hz[...], axis=0) * (1.0 / TOTAL))[:, :M] + known
+    alpha_next_t = nn(inverse1, nt(middle, inverse1))
     coef_ref[2] = alpha_next_t
     residual_ref[...] = image_next - nn(alpha_next_t, second)
 
@@ -358,6 +389,7 @@
             pltpu.VMEM((2, NZ, M, B), F32),
             pltpu.VMEM((2, NZ, M, B), BF16),
             pltpu.VMEM((2, NZ, M, B), BF16),
+            pltpu.VMEM((NZ, M, B), BF16),
             pltpu.VMEM((2, M, B), F32),
             pltpu.VMEM((NZ, 8, B), F32),
             pltpu.VMEM((NZ, 8, B), F32),
@@ -374,7 +406,7 @@
         compiler_params=pltpu.CompilerParams(
             collective_id=0, has_side_effects=True, vmem_limit_bytes=40 << 20
         ),
-    )(coarse_kernel, correlations, neighbor, pair_weight, energies.reshape(1, B), start_block)
+    )(coarse_kernel, correlations, neighbor, pair_weight, energies.reshape(1, B), start_block.T)
     return residual_t.T, jnp.swapaxes(coefficients_t, 1, 2)
 
 

time: 90.1 us -> 73.5 us (0.82)
  Pallas kernels: 86 us -> 66.9 us
  local copies, waits for them, and re-layouts: 2.24 us -> 4.95 us
    pallas_call x1, Pallas kernels: 86 us -> 66.9 us  [on_device(): pl.pallas_call(kernel, out_shape=(jax.ShapeDtypeStruct((M, B), F32), jax....]
    unnamed x11 -> x12, local copies, waits for them, and re-layouts: 2.24 us -> 4.95 us
where the time goes in v2:
time: 73.5 us; the launch traced here: 73.2 us
  Pallas kernels  66.9 us (91%)
  local copies, waits for them, and re-layouts  4.95 us (7%)
  between operations  1.3 us (2%)
    pallas_call x1, Pallas kernels, on_device(): pl.pallas_call(kernel, out_shape=(jax.ShapeDtypeStruct((M, B), F32), jax....  66.9 us
    unnamed x12, local copies, waits for them, and re-layouts  4.95 us

profile of v2, /device:TPU:8, one launch (start us, length us, event | category | flops | bytes accessed | tf_op | source)
XLA Modules:
  0.0 73.2 jit_solution(773442302061116287)
XLA Ops:
  1.3 0.0 copy-start.4
  1.3 0.6 copy-done.4
  1.9 0.0 copy-start
  1.9 0.8 %copy-done = bf16[1,128,128]{2,1,0:T(8,128)(2,1)S(1)} copy-done((bf16[1,128,128]{2,1,0:T(8,128)(2,1)S(1)}, bf16[1,128,128]{2,1,0:T(8,128)(2,1)}, u32[]{:S(2)}) %copy-start) | copy-done | bytes 32792
  2.7 0.0 copy-start.1
  2.7 0.8 %copy-done.1 = f32[128,64]{0,1:T(8,128)S(1)} copy-done((f32[128,64]{0,1:T(8,128)S(1)}, f32[128,64]{0,1:T(8,128)}, u32[]{:S(2)}) %copy-start.1) | copy-done | bytes 32792
  3.4 0.0 copy-start.2
  3.5 0.7 copy-done.2
  4.2 0.0 copy-start.3
  4.2 0.7 copy-done.3
  4.9 66.9 %shard_map.77 = (f32[64,128]{1,0:T(8,128)S(1)}, f32[3,64,64]{2,1,0:T(8,128)S(1)}) custom-call(bf16[64,64]{1,0:T(8,128)(2,1)S(1)} %copy-done.2, bf16[1,128,128]{2,1,0:T(8,128)(2,1)S(1)} %copy-done, s32[1]{0:T(128)S(6)} %copy.10.near_ref, f32[16,256]{1,0:T(8,128)S(1)} %copy-done.3, f32[1,128]{1,0:T(1,128)S(1)} %bitcast.7, f32[64,128]{1,0:T(8,128)S(1)} %bitcast.5), custom_call_target="tpu_custom_call" | custom-call | tf_op jit(solution)/shard_map/pallas_call | solution.py:361
  71.8 0.7 %copy.8 = f32[3,64,64]{2,1,0:T(8,128)} copy(f32[3,64,64]{1,2,0:T(8,128)S(1)} %bitcast.4) | data formatting | bytes 98304
  72.5 0.6 copy.11
Async XLA Ops:
  1.3 0.7 copy-start.4
  1.9 0.8 %copy-start = (bf16[1,128,128]{2,1,0:T(8,128)(2,1)S(1)}, bf16[1,128,128]{2,1,0:T(8,128)(2,1)}, u32[]{:S(2)}) copy-start(bf16[1,128,128]{2,1,0:T(8,128)(2,1)} %corr_ref.1) | copy-start | bytes 98308
  2.7 0.8 %copy-start.1 = (f32[128,64]{0,1:T(8,128)S(1)}, f32[128,64]{0,1:T(8,128)}, u32[]{:S(2)}) copy-start(f32[128,64]{0,1:T(8,128)} %param.11) | copy-start | bytes 98308
  3.4 0.7 copy-start.2
  4.2 0.7 copy-start.3

commit v3 on v2

--- a/solution.py
+++ b/solution.py
@@ -38,10 +38,19 @@
     return lax.broadcasted_iota(jnp.int32, shape, 0)
 
 
+def by_halves(product, a, b):
+    high = a.astype(BF16)
+    low = (a - high.astype(F32)).astype(BF16)
+    both = product(jnp.concatenate([high, low], axis=0), b, None)
+    return both[: a.shape[0]] + both[a.shape[0] :]
+
+
 def packed_product(left, right):
-    twice = jnp.concatenate([right, right], axis=0)
-    upper = nt(left[: M // 2], twice)
-    lower = nt(left[M // 2 :], twice)
+    return packed_rows(nt(left, jnp.concatenate([right, right], axis=0)))
+
+
+def packed_rows(twice):
+    upper, lower = twice[: M // 2], twice[M // 2 :]
     return jnp.where(lanes(upper.shape) < M, upper, lower)
 
 
@@ -130,6 +139,13 @@
         for dx in range(NX)
         if dx or dy
     ]
+    away = sorted(
+        (min(dx, NX - dx) + min(dy, NY - dy), dx, dy) for dy in range(NY) for dx in range(NX)
+    )
+    near_to_far = [
+        [(dx, dy) for hops, dx, dy in away if low <= hops <= high]
+        for low, high in ((0, 0), (1, 1), (2, 2), (3, 4))
+    ]
     count = [0]
     sent = []
     pending = []
@@ -164,9 +180,15 @@
 
     other_half = pl.ds(pl.multiple_of((1 - k) * 32, 32), 32)
     own_half = pl.ds(pl.multiple_of(k * 32, 32), 32)
+    got_gk = push(gk.at[0], gk.at[1], [sibling])
     got_half = push(coarse_ref.at[other_half], chalf, [sibling])
-    got_gk = push(gk.at[0], gk.at[1], [sibling])
     got_near_k = push(near_own, near_k, [sibling])
+    corr = corr_ref[0]
+    start_u = by_halves(nt, start_t, corr)
+
+    got_gk()
+    gxy[me_xy] = gk[0] + gk[1]
+    got_gxy = push(gxy.at[me_xy], gxy.at[me_xy], plane, gxy.at[pl.ds(0, NXY - 1)])
 
     got_half()
     shape = (M, B)
@@ -177,9 +199,6 @@
     mine = cbuf.at[z, yl, x, yh, k]
     got_a = push(mine, mine, z_ring, cbuf.at[pl.ds(0, 7), 0, 0, 0, 0])
 
-    got_gk()
-    gxy[me_xy] = gk[0] + gk[1]
-    got_gxy = push(gxy.at[me_xy], gxy.at[me_xy], plane, gxy.at[pl.ds(0, NXY - 1)])
     got_w = push(weight_ref, w_other, [y_ring[1]])
     near_xy[me_xy] = near_own[...]
     got_near_xy = push(near_xy.at[me_xy], near_xy.at[me_xy], plane, near_xy.at[pl.ds(0, NXY - 1)])
@@ -198,13 +217,24 @@
     gz[z] = jnp.sum(gxy[...], axis=0)
     got_gz = push(gz.at[z], gz.at[z], z_ring, gz.at[pl.ds(0, NZ - 1)])
 
+    def first_part(y_):
+        return cbuf.at[pl.ds(0, 4), y_ % 2, :, y_ // 2, k]
+
+    def second_part(x_):
+        return cbuf.at[pl.ds(4, 4), :, x_, :, k]
+
+    got_c, got_d = [], []
     got_b1()
-    c_first = cbuf.at[pl.ds(0, 4), yl, :, yh, k]
-    c_second = cbuf.at[pl.ds(4, 4), :, x, :, k]
-    fortyeight = cbuf.at[pl.ds(0, 6), :, :, 0, 0]
-    got_c1 = push(c_first, c_first, y_ring, fortyeight)
+    for d in (2, 1, 3):
+        wait = push(first_part(y), first_part(y), [y_ring[d - 1]])
+        got_c.insert(0, (wait, first_part((y - d) % NY)))
     got_b2()
-    got_c2 = push(c_second, c_second, x_ring, fortyeight)
+    for d in (2, 1, 3):
+        wait = push(second_part(x), second_part(x), [x_ring[d - 1]])
+        got_c.insert(0, (wait, second_part((x - d) % NX)))
+    got_c = [got_c[i] for i in (0, 1, 3, 4, 2, 5)]
+    for part in (first_part(y), second_part(x)):
+        got_d.append(push(part, part, [sibling]))
 
     got_w()
     got_near_xy()
@@ -219,40 +249,66 @@
         c.start()
         pending.append(c.wait)
 
-    corr = corr_ref[0].astype(F32)
 
     got_gz()
     gram = unpacked(jnp.sum(gz[...], axis=0) * (1.0 / TOTAL))
     _, inverse0 = factor(gram, fac.at[0])
-    basis = nn(inverse0, start_t)
-
-    def gather(step, vectors):
-        ubuf[step, me_xy] = nt(vectors, corr).astype(BF16)
+
+    def gather(step, images):
+        ubuf[step, me_xy] = images.astype(BF16)
         mine_ = ubuf.at[step, me_xy]
-        return push(mine_, mine_, plane, ubuf.at[step, pl.ds(0, NXY - 1)])
-
-    got_u = gather(0, basis)
+        waits = [None] * 3
+        for g in (2, 1, 0):
+            targets = [device((x + dx) % NX, (y + dy) % NY, z, k) for dx, dy in near_to_far[g + 1]]
+            waits[g] = push(mine_, mine_, targets, ubuf.at[step, pl.ds(0, len(targets))])
+        return waits
+
+    got_u = gather(0, nn(inverse0, start_u))
+    for wait, part in got_c:
+        wait()
+        got_d.append(push(part, part, [sibling]))
     for c in locals_:
         c.wait()
         pending.remove(c.wait)
-    got_c1()
-    got_c2()
-    half_all = cbuf.at[:, :, :, :, k]
-    got_d = push(half_all, half_all, [sibling])
-    got_d()
-    got_u()
-
-    def apply(step):
-        def one_source(q, _):
+    energy = energy_ref[...]
+    basis = nn(inverse0, start_t)
+    first_term = energy * basis
+    first_term_u = by_halves(nt, first_term, corr)
+    corr_gram = nt(corr, corr, None)
+    corr_gram_high = corr_gram.astype(BF16)
+    corr_gram_low = (corr_gram - corr_gram_high.astype(F32)).astype(BF16)
+    for wait in got_d:
+        wait()
+
+    def distance(half, j):
+        return j + 2 if half == 0 else jnp.where(j < 2, j + 6, 3 - j)
+
+    got_r = {0: [], 1: []}
+
+    def send_sums(step, half):
+        targets = {0: (2, 3, 4, 5), 1: (6, 7, 1)}[half]
+        first = 4 * half
+        got_r[step].append(push(
+            lambda i: rsend.at[step, first + i], rbuf.at[step, z],
+            [z_ring[d - 1] for d in targets], rbuf.at[step, pl.ds(0, len(targets))],
+        ))
+
+    def apply(step, got_u, beside=None, between=None):
+        def one_source(dx, dy):
+            q = (y + dy) % NY * NX + (x + dx) % NX
             block = cbuf[near_xy_s[q, 0, 0]].reshape(8, B, B)
             vector = ubuf[step, q]
             for c in range(8):
                 tbuf[q, c] = nn(vector, block[c], None)
-            return 0
-
-        lax.fori_loop(0, NXY, one_source, 0, unroll=4)
-
-        def target(z_, other, out):
+
+        for g, group in enumerate(near_to_far):
+            if g:
+                got_u[g - 1]()
+            for dx, dy in group:
+                one_source(dx, dy)
+
+        def target(d, other):
+            z_ = (z + d) % NZ
             near = near_z_s[z_, other, 0]
             place = z_ * 32 + yh * 16 + yl * 8 + x * 2 + (1 - k if other else k)
             total = jnp.zeros((M, B), F32)
@@ -260,42 +316,57 @@
                 qy, qx = q // NX, q % NX
                 w = w_s[qy // 2, (qy % 2) * 8 + qx * 2 + k, place]
                 total = total + w * tbuf[q, near]
-            out[z_] = total
-
-        def for_sibling(z_, _):
-            target(z_, 1, ysend.at[step])
-            return 0
-
-        def for_own(z_, _):
-            target(z_, 0, ypart)
-            return 0
-
-        lax.fori_loop(0, NZ, for_sibling, 0)
-        got_yk = push(ysend.at[step], yk.at[step], [sibling])
-        lax.fori_loop(0, NZ, for_own, 0)
-        got_yk()
-        total = ypart[...] + yk[step]
-        rsend[step] = total.astype(BF16)
-        got_r = push(
-            lambda d: rsend.at[step, (z + d + 1) % NZ], rbuf.at[step, z], z_ring,
-            rbuf.at[step, pl.ds(0, NZ - 1)],
-        )
+            return total
+
+        got_yk = []
+        for half in (0, 1):
+
+            def for_sibling(j, _, half=half):
+                ysend[step, 4 * half + j] = target(distance(half, j), 1)
+                return 0
+
+            lax.fori_loop(0, 4, for_sibling, 0)
+            part = pl.ds(4 * half, 4)
+            got_yk.append(push(ysend.at[step, part], yk.at[step, part], [sibling]))
+        for half in (0, 1):
+
+            def for_own(j, _, half=half):
+                ypart[4 * half + j] = target(distance(half, j), 0)
+                return 0
+
+            lax.fori_loop(0, 4, for_own, 0)
+            if half == 0 and beside is not None:
+                beside()
+            got_yk[half]()
+            part = pl.ds(4 * half, 4)
+            total = ypart[part] + yk[step, part]
+            rsend[step, part] = total.astype(BF16)
+            if half:
+                own = total[3]
+            if step == 0:
+                send_sums(step, half)
+        if step:
+            between()
+            send_sums(step, 0)
+            send_sums(step, 1)
         rbuf[step, z] = jnp.zeros((M, B), BF16)
-        own = ypart[z] + yk[step, z]
 
         def result():
-            got_r()
-            summed = own + jnp.sum(rbuf[step].astype(F32), axis=0)
-            return nn(summed, corr)
+            for wait in got_r[step]:
+                wait()
+            return own + jnp.sum(rbuf[step].astype(F32), axis=0)
 
         return result
 
-    energy = energy_ref[...]
-    image = energy * basis + apply(0)()
-
-    got_u = gather(1, image)
+    summed = apply(0, got_u)()
+    high = summed.astype(BF16)
+    low = (summed - high.astype(F32)).astype(BF16)
+    twice = nn(jnp.concatenate([high, low], axis=0), corr_gram_high, None)
+    image_u = first_term_u + (twice[:M] + twice[M:] + nn(high, corr_gram_low, None))
+    got_u = gather(1, image_u)
     uz[z] = ubuf[1, me_xy]
     got_uz = push(uz.at[z], uz.at[z], z_ring, uz.at[pl.ds(0, NZ - 1)])
+    image = first_term + by_halves(nn, summed, corr)
     ak[0] = nt(image, jnp.concatenate([basis, image], axis=0))
     got_ak = push(ak.at[0], ak.at[1], [sibling])
     energy_product = packed_product(image, energy * image)
@@ -306,29 +377,35 @@
         lambda d: asend.at[(z + d + 1) % NZ], az.at[z], z_ring, az.at[pl.ds(0, NZ - 1)]
     )
 
-    got_az()
-    axy[me_xy] = jnp.sum(az[...], axis=0)
-    got_axy = push(axy.at[me_xy], axy.at[me_xy], plane, axy.at[pl.ds(0, NXY - 1)])
-    got_u()
-    second_sum = apply(1)
-
-    got_uz()
-    upper = jnp.zeros((M // 2, B), F32)
-    lower = upper
-    for d in range(NZ):
-        twice = jnp.concatenate([rsend[1, d], rsend[1, d]], axis=0)
-        vector = uz[d]
-        upper = upper + nt(vector[: M // 2], twice, None)
-        lower = lower + nt(vector[M // 2 :], twice, None)
-    hsend[...] = energy_product + jnp.where(lanes(upper.shape) < M, upper, lower)
-    got_hk = push(hsend, hk, [sibling])
-    got_axy()
+    got_axy = []
+
+    def beside():
+        got_az()
+        axy[me_xy] = jnp.sum(az[...], axis=0)
+        got_axy.append(
+            push(axy.at[me_xy], axy.at[me_xy], plane, axy.at[pl.ds(0, NXY - 1)])
+        )
+
+    got_hk = []
+
+    def between():
+        got_uz()
+        images = jnp.concatenate(
+            [uz[(z + d) % NZ] for d in (2, 3, 4, 5, 6, 7, 1, 0)], axis=1
+        )
+        sums = jnp.concatenate([rsend[1, i] for i in range(NZ)], axis=1)
+        sums = jnp.concatenate([sums, sums], axis=0)
+        hsend[...] = energy_product + packed_rows(nt(images, sums, None))
+        got_hk.append(push(hsend, hk, [sibling]))
+
+    second_sum = apply(1, got_u, beside, between)
+    got_axy[0]()
     afull[z] = jnp.sum(axy[...], axis=0)
     got_afull = push(afull.at[z], afull.at[z], z_ring, afull.at[pl.ds(0, NZ - 1)])
-    got_hk()
+    got_hk[0]()
     hxy[me_xy] = hsend[...] + hk[...]
     got_hxy = push(hxy.at[me_xy], hxy.at[me_xy], plane, hxy.at[pl.ds(0, NXY - 1)])
-    image_sum = energy * image + second_sum()
+    image_sum = energy * image + by_halves(nn, second_sum(), corr)
     got_hxy()
     hz[z] = jnp.sum(hxy[...], axis=0)
     got_hz = push(hz.at[z], hz.at[z], z_ring, hz.at[pl.ds(0, NZ - 1)])
@@ -345,11 +422,14 @@
     )
     coef_ref[0] = alpha_t
     coef_ref[1] = upper1
+    across = lax.dot_general(
+        inverse1, second, (((0,), (0,)), ((), ())), precision=HIGH, preferred_element_type=F32
+    )
     got_hz()
     middle = unpacked(jnp.sum(hz[...], axis=0) * (1.0 / TOTAL))[:, :M] + known
-    alpha_next_t = nn(inverse1, nt(middle, inverse1))
-    coef_ref[2] = alpha_next_t
-    residual_ref[...] = image_next - nn(alpha_next_t, second)
+    left = nn(inverse1, middle)
+    residual_ref[...] = image_next - nn(left, across)
+    coef_ref[2] = nt(left, inverse1)
 
     for i, like in sent:
         pltpu.make_async_copy(like, like, send.at[i]).wait()
@@ -399,8 +479,8 @@
             pltpu.VMEM((NXY, M // 2, B), F32),
             pltpu.VMEM((NZ, M // 2, B), F32),
             pltpu.VMEM((M // 2, B), F32),
-            pltpu.SemaphoreType.DMA((32,)),
-            pltpu.SemaphoreType.DMA((32,)),
+            pltpu.SemaphoreType.DMA((64,)),
+            pltpu.SemaphoreType.DMA((64,)),
             pltpu.SemaphoreType.DMA((4,)),
         ],
         compiler_params=pltpu.CompilerParams(

time: 73.5 us -> 71.6 us (0.974)
  Pallas kernels: 66.9 us -> 65.1 us
    pallas_call x1, Pallas kernels: 66.9 us -> 65.1 us  [on_device(): pl.pallas_call(kernel, out_shape=(jax.ShapeDtypeStruct((M, B), F32), jax....]
where the time goes in v3:
time: 71.6 us; the launch traced here: 71.3 us
  Pallas kernels  65.1 us (91%)
  local copies, waits for them, and re-layouts  4.95 us (7%)
  between operations  1.3 us (2%)
    pallas_call x1, Pallas kernels, on_device(): pl.pallas_call(kernel, out_shape=(jax.ShapeDtypeStruct((M, B), F32), jax....  65.1 us
    unnamed x12, local copies, waits for them, and re-layouts  4.95 us

profile of v3, /device:TPU:8, one launch (start us, length us, event | category | flops | bytes accessed | tf_op | source)
XLA Modules:
  0.0 71.3 jit_solution(13970651010898439142)
XLA Ops:
  1.3 0.0 copy-start.4
  1.3 0.6 copy-done.4
  1.9 0.0 copy-start
  1.9 0.8 %copy-done = bf16[1,128,128]{2,1,0:T(8,128)(2,1)S(1)} copy-done((bf16[1,128,128]{2,1,0:T(8,128)(2,1)S(1)}, bf16[1,128,128]{2,1,0:T(8,128)(2,1)}, u32[]{:S(2)}) %copy-start) | copy-done | bytes 32792
  2.7 0.0 copy-start.1
  2.7 0.8 %copy-done.1 = f32[128,64]{0,1:T(8,128)S(1)} copy-done((f32[128,64]{0,1:T(8,128)S(1)}, f32[128,64]{0,1:T(8,128)}, u32[]{:S(2)}) %copy-start.1) | copy-done | bytes 32792
  3.4 0.0 copy-start.2
  3.5 0.7 %copy-done.2 = bf16[64,64]{1,0:T(8,128)(2,1)S(1)} copy-done((bf16[64,64]{1,0:T(8,128)(2,1)S(1)}, bf16[64,64]{1,0:T(8,128)(2,1)}, u32[]{:S(2)}) %copy-start.2) | copy-done | bytes 8216
  4.2 0.0 copy-start.3
  4.2 0.7 %copy-done.3 = f32[16,256]{1,0:T(8,128)S(1)} copy-done((f32[16,256]{1,0:T(8,128)S(1)}, f32[16,256]{1,0:T(8,128)}, u32[]{:S(2)}) %copy-start.3) | copy-done | bytes 16408
  4.9 65.1 %shard_map.77 = (f32[64,128]{1,0:T(8,128)S(1)}, f32[3,64,64]{2,1,0:T(8,128)S(1)}) custom-call(bf16[64,64]{1,0:T(8,128)(2,1)S(1)} %copy-done.2, bf16[1,128,128]{2,1,0:T(8,128)(2,1)S(1)} %copy-done, s32[1]{0:T(128)S(6)} %copy.10.near_ref, f32[16,256]{1,0:T(8,128)S(1)} %copy-done.3, f32[1,128]{1,0:T(1,128)S(1)} %bitcast.7, f32[64,128]{1,0:T(8,128)S(1)} %bitcast.5), custom_call_target="tpu_custom_call" | custom-call | tf_op jit(solution)/shard_map/pallas_call | solution.py:441
  69.9 0.7 %copy.8 = f32[3,64,64]{2,1,0:T(8,128)} copy(f32[3,64,64]{1,2,0:T(8,128)S(1)} %bitcast.4) | data formatting | bytes 98304
  70.7 0.6 copy.11
Async XLA Ops:
  1.3 0.7 copy-start.4
  1.9 0.8 %copy-start = (bf16[1,128,128]{2,1,0:T(8,128)(2,1)S(1)}, bf16[1,128,128]{2,1,0:T(8,128)(2,1)}, u32[]{:S(2)}) copy-start(bf16[1,128,128]{2,1,0:T(8,128)(2,1)} %corr_ref.1) | copy-start | bytes 98308
  2.7 0.8 %copy-start.1 = (f32[128,64]{0,1:T(8,128)S(1)}, f32[128,64]{0,1:T(8,128)}, u32[]{:S(2)}) copy-start(f32[128,64]{0,1:T(8,128)} %param.11) | copy-start | bytes 98308
  3.4 0.7 %copy-start.2 = (bf16[64,64]{1,0:T(8,128)(2,1)S(1)}, bf16[64,64]{1,0:T(8,128)(2,1)}, u32[]{:S(2)}) copy-start(bf16[64,64]{1,0:T(8,128)(2,1)} %coarse_ref.1) | copy-start | bytes 24580
  4.2 0.7 %copy-start.3 = (f32[16,256]{1,0:T(8,128)S(1)}, f32[16,256]{1,0:T(8,128)}, u32[]{:S(2)}) copy-start(f32[16,256]{1,0:T(8,128)} %weight_ref.1) | copy-start | bytes 49156

commit v4 on v3

--- a/solution.py
+++ b/solution.py
@@ -112,8 +112,9 @@
 
 
 def kernel(
-    coarse_ref, corr_ref, near_ref, weight_ref, energy_ref, start_ref,
+    coarse_in, corr_in, near_ref, weight_in, energy_in, start_in,
     residual_ref, coef_ref,
+    coarse_ref, corr_ref, weight_ref, energy_ref, start_ref,
     cbuf, chalf, near_k, near_own, near_xy, near_z, near_xy_s, near_z_s, w_other, w_s,
     gk, gxy, gz, gsend, fac,
     ubuf, tbuf, ypart, ysend, yk, rsend, rbuf,
@@ -169,13 +170,25 @@
         pending.append(wait)
         return wait
 
+    loads = [
+        pltpu.make_async_copy(source, place, local.at[4 + i])
+        for i, (source, place) in enumerate((
+            (start_in, start_ref), (coarse_in, coarse_ref), (corr_in, corr_ref),
+            (weight_in, weight_ref), (energy_in, energy_ref),
+        ))
+    ]
+    for load in loads:
+        load.start()
     barrier = pltpu.get_barrier_semaphore()
     partners = [sibling] + plane + z_ring
     for target in partners:
         pl.semaphore_signal(barrier, inc=1, device_id=target, device_id_type=MESH)
     near_own[...] = jnp.full((8, B), near_ref[0], jnp.int32)
+    loads[0].wait()
     start_t = start_ref[...]
     gk[0] = packed_product(start_t, start_t)
+    for load in loads[1:]:
+        load.wait()
     pl.semaphore_wait(barrier, len(partners))
 
     other_half = pl.ds(pl.multiple_of((1 - k) * 32, 32), 32)
@@ -225,14 +238,14 @@
 
     got_c, got_d = [], []
     got_b1()
-    for d in (2, 1, 3):
+    for d in (1, 3, 2):
         wait = push(first_part(y), first_part(y), [y_ring[d - 1]])
-        got_c.insert(0, (wait, first_part((y - d) % NY)))
+        got_c.append((d, wait, first_part((y - d) % NY)))
     got_b2()
-    for d in (2, 1, 3):
+    for d in (1, 3, 2):
         wait = push(second_part(x), second_part(x), [x_ring[d - 1]])
-        got_c.insert(0, (wait, second_part((x - d) % NX)))
-    got_c = [got_c[i] for i in (0, 1, 3, 4, 2, 5)]
+        got_c.append((d, wait, second_part((x - d) % NX)))
+    got_c = [(wait, part) for d, wait, part in sorted(got_c, key=lambda e: e[0] == 2)]
     for part in (first_part(y), second_part(x)):
         got_d.append(push(part, part, [sibling]))
 
@@ -435,18 +448,30 @@
         pltpu.make_async_copy(like, like, send.at[i]).wait()
 
 
+def hand_over(residual_ref, coef_ref, residual_out, coef_out):
+    residual_out[...] = residual_ref[...]
+    for i in range(3):
+        coef_out[i] = coef_ref[i].T
+
+
 def on_device(coarse_kernel, correlations, neighbor, pair_weight, energies, start_block):
     vmem = pl.BlockSpec(memory_space=pltpu.VMEM)
     smem = pl.BlockSpec(memory_space=pltpu.SMEM)
+    hbm = pl.BlockSpec(memory_space=pltpu.HBM)
     residual_t, coefficients_t = pl.pallas_call(
         kernel,
         out_shape=(
             jax.ShapeDtypeStruct((M, B), F32),
             jax.ShapeDtypeStruct((3, M, M), F32),
         ),
-        in_specs=[vmem, vmem, smem, vmem, vmem, vmem],
+        in_specs=[hbm, hbm, smem, hbm, hbm, hbm],
         out_specs=(vmem, vmem),
         scratch_shapes=[
+            pltpu.VMEM((M, M), BF16),
+            pltpu.VMEM((1, B, B), BF16),
+            pltpu.VMEM((16, 256), F32),
+            pltpu.VMEM((1, B), F32),
+            pltpu.VMEM((M, B), F32),
             pltpu.VMEM((8, 2, 4, 2, 2, 32, B), BF16),
             pltpu.VMEM((32, M), BF16),
             pltpu.VMEM((8, B), jnp.int32),
@@ -481,13 +506,22 @@
             pltpu.VMEM((M // 2, B), F32),
             pltpu.SemaphoreType.DMA((64,)),
             pltpu.SemaphoreType.DMA((64,)),
-            pltpu.SemaphoreType.DMA((4,)),
+            pltpu.SemaphoreType.DMA((9,)),
         ],
         compiler_params=pltpu.CompilerParams(
-            collective_id=0, has_side_effects=True, vmem_limit_bytes=40 << 20
+            collective_id=0, has_side_effects=True, vmem_limit_bytes=60 << 20
         ),
     )(coarse_kernel, correlations, neighbor, pair_weight, energies.reshape(1, B), start_block.T)
-    return residual_t.T, jnp.swapaxes(coefficients_t, 1, 2)
+    residual_t, coefficients = pl.pallas_call(
+        hand_over,
+        out_shape=(
+            jax.ShapeDtypeStruct((M, B), F32),
+            jax.ShapeDtypeStruct((3, M, M), F32),
+        ),
+        in_specs=[vmem, vmem],
+        out_specs=(vmem, vmem),
+    )(residual_t, coefficients_t)
+    return residual_t.T, coefficients
 
 
 def solution(mesh):

time: 71.6 us -> 69.1 us (0.965)
  local copies, waits for them, and re-layouts: 4.95 us -> 0 us
  Pallas kernels: 65.1 us -> 67.6 us
    unnamed x12 -> x0, local copies, waits for them, and re-layouts: 4.95 us -> none
    pallas_call x0 -> x1, Pallas kernels: none -> 1.66 us  [on_device(): pl.pallas_call(hand_over, out_shape=(jax.ShapeDtypeStruct((M, B), F32), j...]
    pallas_call x1, Pallas kernels: 65.1 us -> 65.9 us  [on_device(): pl.pallas_call(kernel, out_shape=(jax.ShapeDtypeStruct((M, B), F32), jax....]
where the time goes in v4:
time: 69.1 us; the launch traced here: 68.9 us
  Pallas kernels  67.6 us (98%)
  between operations  1.28 us (2%)
    pallas_call x1, Pallas kernels, on_device(): pl.pallas_call(kernel, out_shape=(jax.ShapeDtypeStruct((M, B), F32), jax....  65.9 us
    pallas_call x1, Pallas kernels, on_device(): pl.pallas_call(hand_over, out_shape=(jax.ShapeDtypeStruct((M, B), F32), j...  1.66 us

profile of v4, /device:TPU:8, one launch (start us, length us, event | category | flops | bytes accessed | tf_op | source)
XLA Modules:
  0.0 68.9 jit_solution(8505966066903539447)
XLA Ops:
  1.3 65.9 %shard_map.77 = (f32[64,128]{1,0:T(8,128)}, f32[3,64,64]{2,1,0:T(8,128)}) custom-call(bf16[64,64]{1,0:T(8,128)(2,1)} %coarse_in.1, bf16[1,128,128]{2,1,0:T(8,128)(2,1)} %corr_in.1, s32[1]{0:T(128)S(6)} %copy.8.near_ref, f32[16,256]{1,0:T(8,128)} %weight_in.1, f32[1,128]{1,0:T(1,128)} %bitcast.4, f32[64,128]{1,0:T(8,128)} %bitcast.3), custom_call_target="tpu_custom_call" | custom-call | tf_op jit(solution)/shard_map/pallas_call | solution.py:461
  67.2 1.7 %shard_map.78 = (f32[64,128]{1,0:T(8,128)}, f32[3,64,64]{2,1,0:T(8,128)}) custom-call(f32[64,128]{1,0:T(8,128)} %get-tuple-element.6.residual_ref, f32[3,64,64]{2,1,0:T(8,128)} %get-tuple-element.7.coef_ref), custom_call_target="tpu_custom_call" | custom-call | tf_op jit(solution)/shard_map/pallas_call | solution.py:515

commit v5 on v4

--- a/solution.py
+++ b/solution.py
@@ -147,6 +147,10 @@
         [(dx, dy) for hops, dx, dy in away if low <= hops <= high]
         for low, high in ((0, 0), (1, 1), (2, 2), (3, 4))
     ]
+    plane_far = [
+        device((x + dx) % NX, (y + dy) % NY, z, k) for hops, dx, dy in away[::-1] if hops
+    ]
+    z_far = [z_ring[d - 1] for d in (4, 3, 5, 2, 6, 1, 7)]
     count = [0]
     sent = []
     pending = []
@@ -201,7 +205,7 @@
 
     got_gk()
     gxy[me_xy] = gk[0] + gk[1]
-    got_gxy = push(gxy.at[me_xy], gxy.at[me_xy], plane, gxy.at[pl.ds(0, NXY - 1)])
+    got_gxy = push(gxy.at[me_xy], gxy.at[me_xy], plane_far, gxy.at[pl.ds(0, NXY - 1)])
 
     got_half()
     shape = (M, B)
@@ -210,14 +214,14 @@
     strip = nn(coarse_ref[own_half, :], place_own, None) + nn(chalf[...], place_sib, None)
     cbuf[z, yl, x, yh, k] = strip.astype(BF16)
     mine = cbuf.at[z, yl, x, yh, k]
-    got_a = push(mine, mine, z_ring, cbuf.at[pl.ds(0, 7), 0, 0, 0, 0])
+    got_a = push(mine, mine, z_far, cbuf.at[pl.ds(0, 7), 0, 0, 0, 0])
 
     got_w = push(weight_ref, w_other, [y_ring[1]])
     near_xy[me_xy] = near_own[...]
-    got_near_xy = push(near_xy.at[me_xy], near_xy.at[me_xy], plane, near_xy.at[pl.ds(0, NXY - 1)])
+    got_near_xy = push(near_xy.at[me_xy], near_xy.at[me_xy], plane_far, near_xy.at[pl.ds(0, NXY - 1)])
     got_near_k()
     near_z[z] = jnp.where(rows((8, B)) == 0, near_own[...], near_k[...])
-    got_near_z = push(near_z.at[z], near_z.at[z], z_ring, near_z.at[pl.ds(0, NZ - 1)])
+    got_near_z = push(near_z.at[z], near_z.at[z], z_far, near_z.at[pl.ds(0, NZ - 1)])
 
     got_a()
     b_first = cbuf.at[pl.ds(0, 4), yl, x, yh, k]
@@ -228,7 +232,7 @@
 
     got_gxy()
     gz[z] = jnp.sum(gxy[...], axis=0)
-    got_gz = push(gz.at[z], gz.at[z], z_ring, gz.at[pl.ds(0, NZ - 1)])
+    got_gz = push(gz.at[z], gz.at[z], z_far, gz.at[pl.ds(0, NZ - 1)])
 
     def first_part(y_):
         return cbuf.at[pl.ds(0, 4), y_ % 2, :, y_ // 2, k]
@@ -299,10 +303,10 @@
     got_r = {0: [], 1: []}
 
     def send_sums(step, half):
-        targets = {0: (2, 3, 4, 5), 1: (6, 7, 1)}[half]
-        first = 4 * half
+        entries = {0: (2, 1, 3, 0), 1: (4, 5, 6)}[half]
+        targets = {0: (4, 3, 5, 2), 1: (6, 7, 1)}[half]
         got_r[step].append(push(
-            lambda i: rsend.at[step, first + i], rbuf.at[step, z],
+            lambda i: rsend.at[step, entries[i]], rbuf.at[step, z],
             [z_ring[d - 1] for d in targets], rbuf.at[step, pl.ds(0, len(targets))],
         ))
 
@@ -378,7 +382,7 @@
     image_u = first_term_u + (twice[:M] + twice[M:] + nn(high, corr_gram_low, None))
     got_u = gather(1, image_u)
     uz[z] = ubuf[1, me_xy]
-    got_uz = push(uz.at[z], uz.at[z], z_ring, uz.at[pl.ds(0, NZ - 1)])
+    got_uz = push(uz.at[z], uz.at[z], z_far, uz.at[pl.ds(0, NZ - 1)])
     image = first_term + by_halves(nn, summed, corr)
     ak[0] = nt(image, jnp.concatenate([basis, image], axis=0))
     got_ak = push(ak.at[0], ak.at[1], [sibling])
@@ -396,7 +400,7 @@
         got_az()
         axy[me_xy] = jnp.sum(az[...], axis=0)
         got_axy.append(
-            push(axy.at[me_xy], axy.at[me_xy], plane, axy.at[pl.ds(0, NXY - 1)])
+            push(axy.at[me_xy], axy.at[me_xy], plane_far, axy.at[pl.ds(0, NXY - 1)])
         )
 
     got_hk = []
@@ -414,14 +418,14 @@
     second_sum = apply(1, got_u, beside, between)
     got_axy[0]()
     afull[z] = jnp.sum(axy[...], axis=0)
-    got_afull = push(afull.at[z], afull.at[z], z_ring, afull.at[pl.ds(0, NZ - 1)])
+    got_afull = push(afull.at[z], afull.at[z], z_far, afull.at[pl.ds(0, NZ - 1)])
     got_hk[0]()
     hxy[me_xy] = hsend[...] + hk[...]
-    got_hxy = push(hxy.at[me_xy], hxy.at[me_xy], plane, hxy.at[pl.ds(0, NXY - 1)])
+    got_hxy = push(hxy.at[me_xy], hxy.at[me_xy], plane_far, hxy.at[pl.ds(0, NXY - 1)])
     image_sum = energy * image + by_halves(nn, second_sum(), corr)
     got_hxy()
     hz[z] = jnp.sum(hxy[...], axis=0)
-    got_hz = push(hz.at[z], hz.at[z], z_ring, hz.at[pl.ds(0, NZ - 1)])
+    got_hz = push(hz.at[z], hz.at[z], z_far, hz.at[pl.ds(0, NZ - 1)])
     got_afull()
     both = afull[...].reshape(M, B) * (1.0 / TOTAL)
     alpha_t = both[:, :M]

time: 69.1 us -> 66.4 us (0.961)
  Pallas kernels: 67.6 us -> 64.8 us
    pallas_call x1, Pallas kernels: 65.9 us -> 63.2 us  [on_device(): pl.pallas_call(kernel, out_shape=(jax.ShapeDtypeStruct((M, B), F32), jax....]
where the time goes in v5:
time: 66.4 us; the launch traced here: 66.1 us
  Pallas kernels  64.8 us (98%)
  between operations  1.28 us (2%)
    pallas_call x1, Pallas kernels, on_device(): pl.pallas_call(kernel, out_shape=(jax.ShapeDtypeStruct((M, B), F32), jax....  63.2 us
    pallas_call x1, Pallas kernels, on_device(): pl.pallas_call(hand_over, out_shape=(jax.ShapeDtypeStruct((M, B), F32), j...  1.66 us

profile of v5, /device:TPU:8, one launch (start us, length us, event | category | flops | bytes accessed | tf_op | source)
XLA Modules:
  0.0 66.1 jit_solution(14409676129752802094)
XLA Ops:
  1.3 63.2 %shard_map.77 = (f32[64,128]{1,0:T(8,128)}, f32[3,64,64]{2,1,0:T(8,128)}) custom-call(bf16[64,64]{1,0:T(8,128)(2,1)} %coarse_in.1, bf16[1,128,128]{2,1,0:T(8,128)(2,1)} %corr_in.1, s32[1]{0:T(128)S(6)} %copy.8.near_ref, f32[16,256]{1,0:T(8,128)} %weight_in.1, f32[1,128]{1,0:T(1,128)} %bitcast.4, f32[64,128]{1,0:T(8,128)} %bitcast.3), custom_call_target="tpu_custom_call" | custom-call | tf_op jit(solution)/shard_map/pallas_call | solution.py:465
  64.4 1.7 %shard_map.78 = (f32[64,128]{1,0:T(8,128)}, f32[3,64,64]{2,1,0:T(8,128)}) custom-call(f32[64,128]{1,0:T(8,128)} %get-tuple-element.6.residual_ref, f32[3,64,64]{2,1,0:T(8,128)} %get-tuple-element.7.coef_ref), custom_call_target="tpu_custom_call" | custom-call | tf_op jit(solution)/shard_map/pallas_call | solution.py:519

commit v6 on v5

--- a/solution.py
+++ b/solution.py
@@ -227,8 +227,8 @@
     b_first = cbuf.at[pl.ds(0, 4), yl, x, yh, k]
     b_second = cbuf.at[pl.ds(4, 4), yl, x, yh, k]
     twelve = cbuf.at[pl.ds(0, 6), :, 0, 0, 0]
-    got_b1 = push(b_first, b_first, x_ring, twelve)
-    got_b2 = push(b_second, b_second, y_ring, twelve)
+    got_b1 = push(b_first, b_first, [x_ring[i] for i in (1, 0, 2)], twelve)
+    got_b2 = push(b_second, b_second, [y_ring[i] for i in (1, 0, 2)], twelve)
 
     got_gxy()
     gz[z] = jnp.sum(gxy[...], axis=0)
@@ -242,11 +242,11 @@
 
     got_c, got_d = [], []
     got_b1()
-    for d in (1, 3, 2):
+    for d in (2, 1, 3):
         wait = push(first_part(y), first_part(y), [y_ring[d - 1]])
         got_c.append((d, wait, first_part((y - d) % NY)))
     got_b2()
-    for d in (1, 3, 2):
+    for d in (2, 1, 3):
         wait = push(second_part(x), second_part(x), [x_ring[d - 1]])
         got_c.append((d, wait, second_part((x - d) % NX)))
     got_c = [(wait, part) for d, wait, part in sorted(got_c, key=lambda e: e[0] == 2)]

time: 66.4 us -> 65.9 us (level)
  no operation moved by 1% of the time
where the time goes in v6:
time: 65.9 us; the launch traced here: 65.6 us
  Pallas kernels  64.3 us (98%)
  between operations  1.28 us (2%)
    pallas_call x1, Pallas kernels, on_device(): pl.pallas_call(kernel, out_shape=(jax.ShapeDtypeStruct((M, B), F32), jax....  62.6 us
    pallas_call x1, Pallas kernels, on_device(): pl.pallas_call(hand_over, out_shape=(jax.ShapeDtypeStruct((M, B), F32), j...  1.66 us

profile of v6, /device:TPU:8, one launch (start us, length us, event | category | flops | bytes accessed | tf_op | source)
XLA Modules:
  0.0 65.6 jit_solution(7091804071349768290)
XLA Ops:
  1.3 62.6 %shard_map.77 = (f32[64,128]{1,0:T(8,128)}, f32[3,64,64]{2,1,0:T(8,128)}) custom-call(bf16[64,64]{1,0:T(8,128)(2,1)} %coarse_in.1, bf16[1,128,128]{2,1,0:T(8,128)(2,1)} %corr_in.1, s32[1]{0:T(128)S(6)} %copy.8.near_ref, f32[16,256]{1,0:T(8,128)} %weight_in.1, f32[1,128]{1,0:T(1,128)} %bitcast.4, f32[64,128]{1,0:T(8,128)} %bitcast.3), custom_call_target="tpu_custom_call" | custom-call | tf_op jit(solution)/shard_map/pallas_call | solution.py:465
  63.9 1.7 %shard_map.78 = (f32[64,128]{1,0:T(8,128)}, f32[3,64,64]{2,1,0:T(8,128)}) custom-call(f32[64,128]{1,0:T(8,128)} %get-tuple-element.6.residual_ref, f32[3,64,64]{2,1,0:T(8,128)} %get-tuple-element.7.coef_ref), custom_call_target="tpu_custom_call" | custom-call | tf_op jit(solution)/shard_map/pallas_call | solution.py:519
